TPU v7x, 128 devices: a whole 4x4x4 slice. The times are simulated.
128 devices in a mesh: atom: 16 (over y, z), fit: 8 (over x, core).
Axes of the slice: x: 4, y: 4, z: 4, core: 2. Of those that a mesh axis runs over, the one named last changes fastest.
Arguments:
- three_centre: bfloat16 [192, 4, 384, 4096], P('atom', None, 'fit'), may hold values from -0.375 to 0.375
- tensor_pattern: int32 [192, 4], P('atom'), may hold values from 0 to 191, all different within a row
- coefficients: bfloat16 [32, 12288], P(None, 'atom'), may hold values from -6 to 6
- readers: int32 [192, 4], replicated, may hold values from 0 to 15, all different within a row; in each aligned block of 12 rows (0 to 11, 12 to 23, ...) at most 6 rows name the same one
Outputs:
- exchange_matrix: bfloat16 [12288, 12288], P(('atom', 'fit'))
Inputs may be any that keep to these rules, and one draw needn't show every extreme that they name: `tensor_pattern`: each row names 4 different blocks, and every block is named by some row. `readers`: each row names 4 different devices, possibly the block's own. Among the 12 blocks of one device (rows b with equal b // 12), no device is named more than 6 times, and in some of these groups a device is named exactly 6 times.
All inputs are finite; a program needn't handle non-finite values.
Results may differ from a plain program's by a relative error of at most 0.0057.
Values may be sent and summed in bfloat16 or wider, within the bound.
No kernel may reach another device: no remote copies, remote signals or barrier semaphores. Data moves between devices by JAX's collectives and lax.ppermute only.
A program may use at most 192 MiB of HBM per device.

v0:
```python
import math

import jax
import jax.numpy as jnp
from jax import lax
from jax.sharding import PartitionSpec as P

BS = 64
KB = 4


def slot_table(selected, capacity):
    before = jnp.cumsum(selected, axis=1) - selected
    places = jnp.arange(capacity, dtype=jnp.int32)
    hit = jnp.logical_and(selected[:, None, :] == 1, before[:, None, :] == places[None, :, None])
    return hit.astype(jnp.int32)


def per_device(three_centre, tensor_pattern, coefficients, readers):
    atom_count = lax.axis_size("atom")
    fit_count = lax.axis_size("fit")
    atom_index = lax.axis_index("atom")
    fit_index = lax.axis_index("fit")
    local_blocks = three_centre.shape[0]
    fit_width = three_centre.shape[2]
    orbital_count = coefficients.shape[0]
    column_width = fit_width * orbital_count
    total_blocks = local_blocks * atom_count
    capacity = local_blocks // 2
    rows_here = local_blocks * BS
    all_coeff = lax.all_gather(coefficients, "atom", axis=1, tiled=True)
    offsets = jnp.arange(BS, dtype=jnp.int32)
    columns = (tensor_pattern[:, :, None] * BS + offsets[None, None, :]).reshape(-1)
    picked = jnp.take(all_coeff, columns, axis=1).reshape(orbital_count, local_blocks, KB, BS)
    tile_rows = three_centre.reshape(local_blocks, KB, fit_width, BS, BS)
    fitted = jnp.einsum("mkplu,imkl->mupi", tile_rows, picked, preferred_element_type=jnp.float32)
    fitted = fitted.astype(jnp.bfloat16).reshape(local_blocks, BS, column_width)
    own_rows = fitted.reshape(rows_here, column_width)
    devices = jnp.arange(atom_count, dtype=jnp.int32)
    block_ids = jnp.arange(local_blocks, dtype=jnp.int32)
    reader_hit = jnp.any(readers[:, None, :] == devices[None, :, None], axis=2).astype(jnp.int32)
    my_readers = lax.dynamic_slice_in_dim(reader_hit, atom_index * local_blocks, local_blocks, 0)
    send_table = slot_table(my_readers.T, capacity)
    incoming = (
        jnp.any(readers == atom_index, axis=1).astype(jnp.int32).reshape(atom_count, local_blocks)
    )
    incoming = incoming * (devices != atom_index).astype(jnp.int32)[:, None]
    recv_table = slot_table(incoming, capacity)
    slot_place = recv_table[:, :, None, :] * jnp.eye(atom_count, dtype=jnp.int32)[:, None, :, None]
    slot_place = slot_place.reshape(atom_count * capacity, total_blocks).astype(jnp.float32)
    own_part = jnp.einsum("rf,cf->rc", own_rows, own_rows, preferred_element_type=jnp.float32)
    slot_source = jnp.sum(send_table * block_ids[None, None, :], axis=2)
    slot_used = jnp.sum(send_table, axis=2)
    outgoing = jnp.take(fitted, slot_source.reshape(-1), axis=0).reshape(
        atom_count, capacity, BS, column_width
    )
    outgoing = outgoing * slot_used.reshape(atom_count, capacity, 1, 1).astype(jnp.bfloat16)
    arrived = lax.all_to_all(outgoing, "atom", split_axis=0, concat_axis=0, tiled=True)
    far_part = jnp.einsum("rf,scbf->rscb", own_rows, arrived, preferred_element_type=jnp.float32)
    far_part = far_part.reshape(rows_here, atom_count * capacity * BS)
    partial_value = jnp.concatenate([own_part, far_part], axis=1)
    shares = lax.psum_scatter(partial_value, "fit", scatter_dimension=0, tiled=True)
    count_rows = shares.shape[0]
    blocks = jnp.arange(total_blocks, dtype=jnp.int32)
    own_place = blocks[None, :] == atom_index * local_blocks + block_ids[:, None]
    placement = jnp.concatenate([own_place.astype(jnp.float32), slot_place], axis=0)
    spread = jnp.einsum(
        "rsb,sn->rnb",
        shares.reshape(count_rows, -1, BS),
        placement,
        precision=lax.Precision.HIGHEST,
    )
    row_ids = fit_index * count_rows + jnp.arange(count_rows, dtype=jnp.int32)
    row_block = atom_index * local_blocks + row_ids // BS
    keep_mask = (row_block[:, None] != blocks[None, :]).astype(jnp.float32)
    scale_factor = 1.0 / math.sqrt(fit_width * fit_count * orbital_count)
    result = spread * keep_mask[:, :, None] * scale_factor
    return result.reshape(count_rows, total_blocks * BS).astype(jnp.bfloat16)


def solution(mesh):
    placed = (P("atom", None, "fit", None), P("atom", None), P(None, "atom"), P())
    return jax.shard_map(
        per_device, mesh=mesh, in_specs=placed, out_specs=P(("atom", "fit"), None), check_vma=False
    )
```

profile of v0, /device:TPU:1, one launch (start us, length us, event | category | flops | bytes accessed | tf_op | source)
XLA Modules:
  0.0 676.1 jit_solution(780923290783337366)
XLA Ops:
  6.5 0.7 broadcast_multiply_fusion
  7.5 0.7 fusion.16
  9.0 50.8 %reshape.231 = bf16[12,4,48,64,64]{4,3,2,1,0:T(8,128)(2,1)} reshape(bf16[12,4,48,4096]{3,2,1,0:T(8,128)(2,1)} %param.4) | data formatting | bytes 37748736 | tf_op jit(solution)/shard_map/reshape | solution.py:35
  59.9 28.2 %all_gather.3 = bf16[32,12288]{0,1:T(8,128)(2,1)S(1)} all-gather(bf16[32,768]{0,1:T(8,128)(2,1)S(1)} %copy.29), channel_id=1, replica_groups=mesh['atom'=16,'fit'=8] {'atom'}, dimensions={1}, use_global_device_ids=true | all-gather | bytes 835584 | tf_op jit(solution)/shard_map/all_gather | solution.py:31
  88.2 11.5 %gather_fusion = bf16[3072,32]{1,0:T(8,128)(2,1)} fusion(bf16[32,12288]{0,1:T(8,128)(2,1)S(1)} %all_gather.3, s32[3072]{0:T(1024)S(1)} %broadcast_clamp_fusion), kind=kCustom, calls=%fused_computation | custom fusion | bytes 405504 | tf_op jit(solution)/shard_map/jit(_take)/gather | solution.py:34
  99.8 1.4 copy.30
  101.3 17.5 %bitcast_convert_fusion = bf16[12,32,48,64]{3,1,2,0:T(8,128)(2,1)} fusion(bf16[12,4,48,64,64]{4,3,2,1,0:T(8,128)(2,1)} %reshape.231, bf16[32,12,4,64]{3,0,2,1:T(8,128)(2,1)S(1)} %copy.30, pred[12,4,64]{2,1,0:T(4,128)(4,1)S(1)} %compare_and_fusion), kind=kOutput, calls=%fused_computation.4 | convolution fusion | flops 605257728 | bytes 21433344 | tf_op jit(solution)/shard_map/mkplu,imkl->mupi/dot_general | solution.py:36
  118.8 16.5 %gather_fusion.1 = bf16[96,64,1536]{1,2,0:T(8,128)(2,1)} fusion(bf16[12,64,1536]{1,2,0:T(8,128)(2,1)} %bitcast.51, s32[1024]{0:T(1024)S(1)} %pad_clamp_fusion), kind=kCustom, calls=%fused_computation.1 | custom fusion | bytes 37749120 | tf_op jit(solution)/shard_map/jit(_take)/gather | solution.py:54
  135.3 34.2 %copy.35 = bf16[96,64,1536]{2,1,0:T(8,128)(2,1)} copy(bf16[96,64,1536]{1,2,0:T(8,128)(2,1)} %gather_fusion.1) | data formatting | bytes 37748736 | tf_op jit(solution)/shard_map/jit(_take)/gather | solution.py:54
  169.7 17.5 %select_multiply_fusion = bf16[16,6,64,1536]{3,2,1,0:T(8,128)(2,1)} fusion(bf16[16,6,64,1536]{3,2,1,0:T(8,128)(2,1)} %bitcast.53, pred[16,6]{1,0:T(8,128)(4,1)S(1)} %copy.33, bf16[16,6]{1,0:T(8,128)(2,1)S(1)} %copy.36), kind=kLoop, calls=%fused_computation.3 | loop fusion | flops 18874368 | bytes 37749024 | tf_op jit(solution)/shard_map/mul | solution.py:57
  187.2 5.2 all-to-all-start
  192.5 9.8 %copy.32 = bf16[12,64,48,32]{1,0,3,2:T(8,128)(2,1)} copy(bf16[12,64,48,32]{1,3,2,0:T(8,128)(2,1)} %bitcast.52) | data formatting | bytes 4718592 | tf_op jit(solution)/shard_map/convert_element_type | solution.py:37
  202.3 7.2 %reshape_reshape.3 = bf16[768,1536]{0,1:T(8,128)(2,1)S(1)} reshape(bf16[12,64,48,32]{1,0,3,2:T(8,128)(2,1)} %copy.32) | data formatting | bytes 4718592 | tf_op jit(solution)/shard_map/reshape;reshape | solution.py:38
  209.6 3.5 fusion.25
  213.0 278.0 %all-to-all-done = bf16[16,6,64,1536]{3,2,1,0:T(8,128)(2,1)} async-done(((bf16[16,6,64,1536]{3,2,1,0:T(8,128)(2,1)}), bf16[16,6,64,1536]{3,2,1,0:T(8,128)(2,1)}, u32[]{:S(2)}, u32[]{:S(2)}) %all-to-all-start) | async-done | bytes 18874400 | tf_op jit(solution)/shard_map/all_to_all | solution.py:58
  491.0 20.9 %fusion.26 = f32[768,6144]{1,0:T(8,128)} fusion(bf16[768,1536]{0,1:T(8,128)(2,1)S(1)} %reshape_reshape.3, bf16[6144,1536]{1,0:T(8,128)(2,1)} %bitcast.13), kind=kOutput, calls=%fused_computation.61 | convolution fusion | flops 14495514624 | bytes 40108032 | tf_op jit(solution)/shard_map/rf,scbf->rscb/dot_general | solution.py:59
  511.9 14.1 %pad_maximum_fusion = f32[768,6912]{1,0:T(8,128)} fusion(f32[768,6144]{1,0:T(8,128)} %fusion.26, f32[768,768]{1,0:T(8,128)S(1)} %copy-done), kind=kLoop, calls=%fused_computation.2 | loop fusion | flops 5308416 | bytes 42467328 | tf_op jit(solution)/shard_map/concatenate | solution.py:61
  526.0 0.7 copy-done.2
  527.7 0.7 copy.27
  529.7 122.3 %reduce-scatter.2.cloned.1.call-done = f32[96,6912]{1,0:T(8,128)} async-done(((f32[768,6912]{1,0:T(8,128)}), f32[96,6912]{1,0:T(8,128)}) %reduce-scatter.2.cloned.1.call-update) | async-done | bytes 2654224 | tf_op jit(solution)/shard_map/reduce_scatter | solution.py:62
  652.1 2.4 copy.38
  654.5 10.1 %fusion.1 = bf16[96,192,64]{0,1,2:T(8,128)(2,1)S(1)} fusion(f32[96,192]{0,1:T(8,128)} %fusion.13, f32[96,108,64]{0,2,1:T(8,128)S(1)} %bitcast.54, f32[96,192]{0,1:T(8,128)} %copy.27, f32[12,192]{0,1:T(8,128)} %fusion.12), kind=kOutput, calls=%fused_computation.7 | convolution fusion | flops 1532383488 | bytes 5170176 | tf_op jit(solution)/shard_map/rsb,sn->rnb/dot_general | solution.py:67
  664.6 2.0 copy.40
  666.6 2.6 copy.41
  (42 shorter events, 4.0 us)
Async XLA Ops:
  9.0 50.8 %copy-start.1 = (bf16[32,768]{1,0:T(8,128)(2,1)S(1)}, bf16[32,768]{1,0:T(8,128)(2,1)}, u32[]{:S(2)}) copy-start(bf16[32,768]{1,0:T(8,128)(2,1)} %param.6) | copy-start | bytes 147460
  187.2 303.8 %all-to-all-start = ((bf16[16,6,64,1536]{3,2,1,0:T(8,128)(2,1)}), bf16[16,6,64,1536]{3,2,1,0:T(8,128)(2,1)}, u32[]{:S(2)}, u32[]{:S(2)}) async-start(bf16[16,6,64,1536]{3,2,1,0:T(8,128)(2,1)} %select_multiply_fusion), calls=%async_computation | async-start | bytes 37748736 | tf_op jit(solution)/shard_map/all_to_all | solution.py:58
  192.4 459.7 %reduce-scatter.2.cloned.1.call-start = ((), (), s32[]{:S(2)}) async-start(), calls=%async_computation.2 | async-start | bytes 23887872 | tf_op jit(solution)/shard_map/reduce_scatter | solution.py:62
  491.0 20.9 %copy-start = (f32[768,768]{1,0:T(8,128)S(1)}, f32[768,768]{1,0:T(8,128)}, u32[]{:S(2)}) copy-start(f32[768,768]{1,0:T(8,128)} %fusion.25) | copy-start | bytes 7077892
  526.0 0.7 copy-start.2
Sparse Core Ops, SparseCore 0:
  526.1 125.9 reduce-scatter.1
where the time goes:
time: 679 us; the launch traced here: 676 us
  waiting for transfers between devices  400 us (59%)
  local copies, waits for them, and re-layouts  141 us (21%)
  matrix products  51.9 us (8%)
  other arithmetic  35.7 us (5%)
  blocking collectives  28.2 us (4%)
  between operations  13.6 us (2%)
    all_to_all x1, waiting for transfers between devices, per_device(): lax.all_to_all(outgoing, 'atom', split_axis=0, concat_axis=0, tiled=True)  278 us
    reduce_scatter x1, waiting for transfers between devices, per_device(): lax.psum_scatter(partial_value, 'fit', scatter_dimension=0, tiled=True)  122 us
    reshape x1, local copies, waits for them, and re-layouts, per_device(): tile_rows = three_centre.reshape(local_blocks, KB, fit_width, BS, BS)  50.8 us
    gather x2, local copies, waits for them, and re-layouts, per_device(): jnp.take(fitted, slot_source.reshape(-1), axis=0)  50.7 us
    all_gather x1, blocking collectives, per_device(): all_coeff = lax.all_gather(coefficients, 'atom', axis=1, tiled=True)  28.2 us
    dot_general x1, matrix products, per_device(): jnp.einsum('rf,scbf->rscb', own_rows, arrived, preferred_element_type=jnp...  20.9 us
    mul x1, other arithmetic, per_device(): outgoing * slot_used.reshape(atom_count, capacity, 1, 1).astype(jnp.bfloa...  17.5 us
    dot_general x1, matrix products, per_device(): jnp.einsum('mkplu,imkl->mupi', tile_rows, picked, preferred_element_type=...  17.5 us
  transfers between devices with their start and end apart: 2, of which 2 were waited for; matrix products, arithmetic and copies ran while one was open for 3% of the time, Pallas kernels for 0%

commit v1 on v0

v1 whole, which is shorter than its diff:
```python
import functools
import math

import jax
import jax.numpy as jnp
import numpy as np
from jax import lax
from jax.experimental import pallas as pl
from jax.experimental.pallas import tpu as pltpu
from jax.sharding import PartitionSpec as P

BS = 64
KB = 4
NBD = 12
CAP = 6
NP = 48
NOCC = 32
HALF = NP * NOCC // 2
SIDE = 4
FIT = 8
ROWS = NBD * BS
PIECE = ROWS // FIT
MIB = 2**20

STEP = {"+y": (1, 0), "-y": (3, 0), "+z": (0, 1), "-z": (0, 3)}
PLAN = (
    (1, 1, (1, 0), (0, 0), "+y", True),
    (1, 0, (0, 1), (0, 0), "+z", True),
    (1, 1, (3, 0), (0, 0), "-y", False),
    (1, 0, (3, 0), (0, 0), "-y", False),
    (1, 0, (0, 3), (0, 0), "-z", True),
    (2, 0, (1, 1), (0, 1), "+y", True),
    (2, 1, (1, 1), (1, 0), "+z", True),
    (2, 0, (3, 3), (0, 3), "-y", True),
    (2, 1, (0, 3), (0, 0), "-z", True),
    (3, 0, (1, 3), (0, 3), "+y", False),
    (3, 0, (1, 0), (0, 0), "+y", False),
    (3, 1, (0, 1), (0, 0), "+z", False),
    (3, 0, (0, 2), (0, 1), "+z", False),
    (3, 1, (3, 3), (0, 3), "-y", True),
    (3, 1, (0, 2), (0, 3), "-z", False),
    (3, 1, (1, 3), (1, 0), "-z", False),
    (4, 1, (2, 1), (1, 1), "+y", True),
    (4, 1, (1, 2), (1, 1), "+z", False),
    (4, 0, (1, 2), (1, 1), "+z", False),
    (4, 0, (2, 3), (3, 3), "-y", True),
    (4, 1, (3, 2), (3, 3), "-z", False),
    (4, 0, (3, 2), (3, 3), "-z", False),
    (5, 0, (2, 1), (1, 1), "+y", False),
    (5, 1, (3, 1), (2, 1), "+y", False),
    (5, 1, (2, 2), (2, 1), "+z", False),
    (5, 0, (2, 0), (2, 3), "+z", False),
    (5, 0, (3, 1), (0, 1), "-y", False),
    (5, 1, (2, 3), (3, 3), "-y", False),
    (5, 0, (2, 2), (2, 3), "-z", False),
    (5, 1, (2, 0), (2, 1), "-z", False),
)
OFFSETS = tuple(
    sorted({p[2] for p in PLAN}, key=lambda o: (max(p[0] for p in PLAN if p[2] == o), o))
)
DONE = {o: max(p[0] for p in PLAN if p[2] == o) for o in OFFSETS}
CHUNKS = (
    tuple(o for o in OFFSETS if DONE[o] <= 3),
    tuple(o for o in OFFSETS if DONE[o] > 3),
)
TILES = CAP // 2
OWN_TILES = NBD // 2
BASE = {(0, 0): 0}
for _o in CHUNKS[0] + CHUNKS[1]:
    BASE[_o] = OWN_TILES + TILES * (len(BASE) - 1)
COUNT = (OWN_TILES + TILES * len(CHUNKS[0]), TILES * len(CHUNKS[1]))


def minus(a, b):
    return ((a[0] - b[0]) % SIDE, (a[1] - b[1]) % SIDE)


def plus(a, b):
    return ((a[0] + b[0]) % SIDE, (a[1] + b[1]) % SIDE)


def number(a):
    return a[0] * SIDE + a[1]


PLACES = tuple((y, z) for y in range(SIDE) for z in range(SIDE))
LEAVES = tuple(p for p in PLAN if not p[5])
PAIRS = np.array(
    [
        [(number(minus(me, o)), number(me)) for o in OFFSETS]
        + [
            (number(minus(plus(me, STEP[p[4]]), p[2])), number(plus(me, STEP[p[4]])))
            for p in LEAVES
        ]
        for me in PLACES
    ],
    dtype=np.int32,
)
BASE_OF = np.array([[BASE[minus(me, h)] for h in PLACES] for me in PLACES], dtype=np.int32)


def fit_kernel(tile_ref, coeff_ref, first_ref, second_ref, lines):
    for m in range(2):
        for k in range(KB):
            for pair in range(BS // 2):
                value = tile_ref[m, k, :, pair * 128 : (pair + 1) * 128]
                lines[m, pl.ds((k * 32 + pair) * NP, NP), :] = value.astype(jnp.float32)
    for group in range(NP // 4):
        both = []
        for m in range(2):
            parts = []
            for p in range(group * 4, group * 4 + 4):
                rows = lines[m, pl.ds(p, 128, stride=NP), :].astype(jnp.bfloat16)
                product = jnp.dot(coeff_ref[m], rows, preferred_element_type=jnp.float32)
                parts.append(product[0:NOCC] + pltpu.roll(product[NOCC:], 64, 1))
            both.append(jnp.concatenate(parts, axis=0)[:, 0:BS])
        turned = jnp.concatenate(both, axis=1).T.astype(jnp.bfloat16)
        out_ref = first_ref if group < 6 else second_ref
        place = (group % 6) * 128
        out_ref[0, :, place : place + 128] = turned[0:BS]
        out_ref[1, :, place : place + 128] = turned[BS:]


def fit_rows(three_centre, picked):
    out = jax.ShapeDtypeStruct((NBD, BS, HALF), jnp.bfloat16)
    return pl.pallas_call(
        fit_kernel,
        grid=(NBD // 2,),
        in_specs=[
            pl.BlockSpec((2, KB, NP, BS * BS), lambda g: (g, 0, 0, 0)),
            pl.BlockSpec((2, 2 * NOCC, 128), lambda g: (g, 0, 0)),
        ],
        out_specs=[pl.BlockSpec((2, BS, HALF), lambda g: (g, 0, 0))] * 2,
        out_shape=[out, out],
        scratch_shapes=[pltpu.VMEM((2, KB * 32 * NP, 128), jnp.float32)],
        compiler_params=pltpu.CompilerParams(vmem_limit_bytes=40 * MIB),
    )(three_centre, picked)


def pack_kernel(index_ref, left_ref, right_ref, out_ref):
    step = pl.program_id(0)

    @pl.when(step < CAP)
    def _():
        out_ref[...] = left_ref[...]

    @pl.when(step >= CAP)
    def _():
        out_ref[...] = right_ref[...]


def pack(left, right, index):
    block = (1, BS, HALF)
    return pl.pallas_call(
        pack_kernel,
        grid_spec=pltpu.PrefetchScalarGridSpec(
            num_scalar_prefetch=1,
            grid=(2 * CAP,),
            in_specs=[
                pl.BlockSpec(block, lambda s, ix: (ix[jnp.minimum(s, CAP - 1)], 0, 0)),
                pl.BlockSpec(block, lambda s, ix: (ix[jnp.maximum(s, CAP)], 0, 0)),
            ],
            out_specs=pl.BlockSpec(block, lambda s, ix: (s, 0, 0)),
        ),
        out_shape=jax.ShapeDtypeStruct((NBD, BS, HALF), jnp.bfloat16),
        compiler_params=pltpu.CompilerParams(vmem_limit_bytes=16 * MIB),
        cost_estimate=pl.CostEstimate(flops=0, bytes_accessed=5 * MIB, transcendentals=0),
    )(index, left, right)


def product_kernel(scale, index_ref, own_a, own_b, far_a, far_b, _, out_ref, side_a, side_b):
    @pl.when(pl.program_id(0) == 0)
    def _():
        for s in range(CAP):
            side_a[s * BS : (s + 1) * BS, :] = far_a[index_ref[s]]
            side_b[s * BS : (s + 1) * BS, :] = far_b[index_ref[CAP + s]]

    last = (((1,), (1,)), ((), ()))
    total = lax.dot_general(own_a[...], side_a[...], last, preferred_element_type=jnp.float32)
    total += lax.dot_general(own_b[...], side_b[...], last, preferred_element_type=jnp.float32)
    total = (total * scale).astype(jnp.bfloat16)
    for f in range(FIT // 2):
        for t in range(TILES):
            out_ref[f, t] = total[f * PIECE : (f + 1) * PIECE, t * 128 : (t + 1) * 128]


def product(own, far, index, buffer, tile, count, scale):
    whole = pl.BlockSpec((NBD, BS, HALF), lambda m, ix: (0, 0, 0))
    rows = pl.BlockSpec((ROWS // 2, HALF), lambda m, ix: (m, 0))
    shape = jax.ShapeDtypeStruct((FIT, count, PIECE, 128), jnp.bfloat16)
    if buffer is None:
        given, aliases = [], {}
    else:
        given, aliases = [buffer], {5: 0}
    kernel = functools.partial(product_kernel, scale)
    if buffer is None:
        inner = kernel
        kernel = lambda ix, a, b, c, d, *rest: inner(ix, a, b, c, d, None, *rest)
    return pl.pallas_call(
        kernel,
        grid_spec=pltpu.PrefetchScalarGridSpec(
            num_scalar_prefetch=1,
            grid=(2,),
            in_specs=[rows, rows, whole, whole] + [pl.BlockSpec(memory_space=pl.ANY)] * len(given),
            out_specs=pl.BlockSpec(
                (FIT // 2, TILES, PIECE, 128), lambda m, ix: (m, tile // TILES, 0, 0)
            ),
            scratch_shapes=[pltpu.VMEM((CAP * BS, HALF), jnp.bfloat16)] * 2,
        ),
        out_shape=shape,
        input_output_aliases=aliases,
        compiler_params=pltpu.CompilerParams(vmem_limit_bytes=24 * MIB),
        cost_estimate=pl.CostEstimate(
            flops=2 * ROWS * CAP * BS * 2 * HALF, bytes_accessed=6 * MIB, transcendentals=0
        ),
    )(index, own[0].reshape(ROWS, HALF), own[1].reshape(ROWS, HALF), far[0], far[1], *given)


def place_kernel(source_ref, here_ref, first_ref, second_ref, out_ref):
    lane = lax.broadcasted_iota(jnp.int32, (PIECE, 128), 1)
    line = lax.broadcasted_iota(jnp.int32, (PIECE, 128), 0)
    row_block = here_ref[0] * NBD + ((line + here_ref[1] * PIECE) >> 6)

    def fetch(slot):
        tile = jnp.maximum(slot, 0) >> 1
        near = first_ref[0, jnp.minimum(tile, COUNT[0] - 1)]
        far = second_ref[0, jnp.clip(tile - COUNT[0], 0, COUNT[1] - 1)]
        return jnp.where(tile < COUNT[0], near, far).astype(jnp.float32)

    def one(pair, _):
        left, right = source_ref[2 * pair], source_ref[2 * pair + 1]
        a, b = fetch(left), fetch(right)
        a = jnp.where((left & 1) == 1, pltpu.roll(a, 64, 1), a)
        b = jnp.where((right & 1) == 0, pltpu.roll(b, 64, 1), b)
        a = jnp.where(left < 0, 0.0, a)
        b = jnp.where(right < 0, 0.0, b)
        value = jnp.where(lane < 64, a, b)
        block = 2 * pair + (lane >> 6)
        value = jnp.where(row_block == block, 0.0, value)
        out_ref[:, pl.ds(pl.multiple_of(pair * 128, 128), 128)] = value.astype(jnp.bfloat16)
        return 0

    lax.fori_loop(0, SIDE * SIDE * NBD // 2, one, 0)


def place(source, here, first, second):
    smem = pl.BlockSpec(memory_space=pltpu.SMEM)
    vmem = pl.BlockSpec(memory_space=pltpu.VMEM)
    return pl.pallas_call(
        place_kernel,
        in_specs=[smem, smem, vmem, vmem],
        out_specs=vmem,
        out_shape=jax.ShapeDtypeStruct((PIECE, SIDE * SIDE * NBD * BS), jnp.bfloat16),
        compiler_params=pltpu.CompilerParams(vmem_limit_bytes=24 * MIB),
    )(source, here, first, second)


def per_device(three_centre, tensor_pattern, coefficients, readers):
    groups = SIDE * SIDE
    me = lax.axis_index("atom")
    lane = lax.axis_index("fit")
    mine = coefficients.reshape(NOCC, NBD, 32, 2).transpose(1, 3, 0, 2).reshape(NBD, 2 * NOCC, 32)
    everyone = lax.all_to_all(
        jnp.broadcast_to(mine[None], (groups,) + mine.shape), "atom", 0, 0, tiled=True
    ).reshape(groups * NBD, 2 * NOCC, 32)
    picked = jnp.take(everyone, tensor_pattern.reshape(-1), axis=0)
    picked = picked.reshape(NBD, KB, 2 * NOCC, 32).transpose(0, 2, 1, 3).reshape(NBD, 2 * NOCC, 128)
    own = fit_rows(three_centre, picked)

    by_group = readers.reshape(groups, NBD, 4)
    pairs = jnp.asarray(PAIRS)[me]
    hit = jnp.any(by_group[pairs[:, 0]] == pairs[:, 1][:, None, None], axis=2)
    numbers = jnp.arange(NBD, dtype=jnp.int32)
    earlier = numbers[:, None] < numbers[None, :]
    rank = jnp.sum((hit[:, :, None] & earlier[None]).astype(jnp.int32), axis=1)
    slots = jnp.arange(CAP, dtype=jnp.int32)
    chosen = hit[:, None, :] & (rank[:, None, :] == slots[None, :, None])
    lists = jnp.sum(chosen.astype(jnp.int32) * numbers[None, None, :], axis=2)
    reads = jnp.any(by_group == me, axis=2)
    read_rank = jnp.sum((reads[:, :, None] & earlier[None]).astype(jnp.int32), axis=1)
    source = jnp.where(reads, 2 * jnp.asarray(BASE_OF)[me][:, None] + read_rank, -1)
    source = jnp.where(jnp.arange(groups)[:, None] == me, numbers[None, :], source).reshape(-1)

    held = {(0, (0, 0)): (own[0], None), (1, (0, 0)): (own[1], None)}
    for turn in range(1, 6):
        arrived = {}
        for way, step in STEP.items():
            jobs = [p for p in PLAN if p[0] == turn and p[4] == way]
            if not jobs:
                continue
            if jobs[0][5]:
                payload = held[jobs[0][1], jobs[0][3]][0]
            else:
                rows = [lists[len(OFFSETS) + LEAVES.index(p)] for p in jobs]
                payload = pack(
                    held[jobs[0][1], jobs[0][3]][0],
                    held[jobs[1][1], jobs[1][3]][0],
                    jnp.concatenate(rows),
                )
            route = [(number(a), number(plus(a, step))) for a in PLACES]
            landed = lax.ppermute(payload, "atom", route)
            for position, p in enumerate(jobs):
                arrived[p[1], p[2]] = (landed, None if p[5] else position)
        held.update(arrived)

    scale = 1.0 / math.sqrt(FIT * 2 * HALF)
    shares = []
    for number_of, chunk in enumerate(CHUNKS):
        buffer = None
        first_tile = 0 if number_of == 0 else COUNT[0]
        jobs = []
        if number_of == 0:
            for part in range(2):
                index = np.tile(np.arange(part * CAP, (part + 1) * CAP, dtype=np.int32), 2)
                jobs.append((own, jnp.asarray(index), part * TILES))
        for o in chunk:
            far = [held[half, o] for half in range(2)]
            row = lists[OFFSETS.index(o)]
            index = [row if at is None else slots + at * CAP for _, at in far]
            jobs.append(((far[0][0], far[1][0]), jnp.concatenate(index), BASE[o] - first_tile))
        for far, index, tile in jobs:
            buffer = product(own, far, index, buffer, tile, COUNT[number_of], scale)
        shares.append(lax.psum_scatter(buffer, "fit", scatter_dimension=0, tiled=True))
    return place(source, jnp.stack([me, lane]).astype(jnp.int32), shares[0], shares[1])


def solution(mesh):
    placed = (P("atom", None, "fit", None), P("atom", None), P(None, "atom"), P())
    return jax.shard_map(
        per_device, mesh=mesh, in_specs=placed, out_specs=P(("atom", "fit"), None), check_vma=False
    )
```

time: 679 us -> 320 us (0.47)
  waiting for transfers between devices: 400 us -> 149 us
  local copies, waits for them, and re-layouts: 141 us -> 20.1 us
  Pallas kernels: 0 us -> 95.4 us
  matrix products: 51.9 us -> 0 us
  other arithmetic: 35.7 us -> 4.03 us
  starting transfers between devices: 5.26 us -> 34.8 us
  blocking collectives: 28.2 us -> 0 us
    all_to_all x1, waiting for transfers between devices: 278 us -> 12.4 us  [per_device(): lax.all_to_all(jnp.broadcast_to(mine[None], (groups,) + mine.shape), 'ato...]
    pallas_call x0 -> x29, Pallas kernels: none -> 95.4 us  [the longest x17 44.4 us: product(): pl.pallas_call(kernel, grid_spec=pltpu.PrefetchScalarGridSpec(num_scalar_...]
    ppermute x0 -> x20, waiting for transfers between devices: none -> 92.5 us  [per_device(): landed = lax.ppermute(payload, 'atom', route)]
    reduce_scatter x1 -> x2, waiting for transfers between devices: 122 us -> 44.1 us  [per_device(): lax.psum_scatter(buffer, 'fit', scatter_dimension=0, tiled=True)]
    gather x4 -> x2, local copies, waits for them, and re-layouts: 63.7 us -> 2.62 us  [the longest x1 2 us: per_device(): hit = jnp.any(by_group[pairs[:, 0]] == pairs[:, 1][:, None, None], axis=2)]
    dot_general x4 -> x0, matrix products: 51.9 us -> none  [the longest x1 20.9 us: per_device(): jnp.einsum('rf,scbf->rscb', own_rows, arrived, preferred_element_type=jnp...]
    reshape x2 -> x4, local copies, waits for them, and re-layouts: 50.9 us -> 2.34 us  [the longest x2 2.07 us: per_device(): by_group = readers.reshape(groups, NBD, 4)]
    all_gather x1 -> x0, blocking collectives: 28.2 us -> none  [per_device(): all_coeff = lax.all_gather(coefficients, 'atom', axis=1, tiled=True)]
  transfers between devices with their start and end apart: 2 -> 23, of which waited for: 2 -> 10; matrix products, arithmetic and copies ran while one was open for 3% -> 4% of each run, Pallas kernels for 0% -> 19%
where the time goes in v1:
time: 320 us; the launch traced here: 317 us
  waiting for transfers between devices  149 us (47%)
  Pallas kernels  95.4 us (30%)
  starting transfers between devices  34.8 us (11%)
  local copies, waits for them, and re-layouts  20.1 us (6%)
  between operations  14 us (4%)
  other arithmetic  4.03 us (1%)
    ppermute x20, waiting for transfers between devices, per_device(): landed = lax.ppermute(payload, 'atom', route)  92.5 us
    pallas_call x17, Pallas kernels, product(): pl.pallas_call(kernel, grid_spec=pltpu.PrefetchScalarGridSpec(num_scalar_...  44.4 us
    reduce_scatter x2, waiting for transfers between devices, per_device(): lax.psum_scatter(buffer, 'fit', scatter_dimension=0, tiled=True)  44.1 us
    ppermute x20, starting transfers between devices, per_device(): landed = lax.ppermute(payload, 'atom', route)  26 us
    pallas_call x10, Pallas kernels, pack(): pl.pallas_call(pack_kernel, grid_spec=pltpu.PrefetchScalarGridSpec(num_sc...  20.6 us
    pallas_call x1, Pallas kernels, fit_rows(): pl.pallas_call(fit_kernel, grid=(NBD // 2,), in_specs=[pl.BlockSpec((2, K...  19.1 us
    all_to_all x1, waiting for transfers between devices, per_device(): lax.all_to_all(jnp.broadcast_to(mine[None], (groups,) + mine.shape), 'ato...  12.4 us
    unnamed x49, local copies, waits for them, and re-layouts  11.6 us
  transfers between devices with their start and end apart: 23, of which 10 were waited for; matrix products, arithmetic and copies ran while one was open for 4% of the time, Pallas kernels for 19%

profile of v1, /device:TPU:1, one launch (start us, length us, event | category | flops | bytes accessed | tf_op | source)
XLA Modules:
  0.0 317.4 jit_solution(17656969239167041303)
XLA Ops:
  9.8 8.7 %all-to-all-start = ((bf16[16,2,12288]{2,1,0:T(2,128)(2,1)}), bf16[16,2,12288]{2,1,0:T(2,128)(2,1)S(1)}, u32[]{:S(2)}, u32[]{:S(2)}) async-start(bf16[16,2,12288]{2,1,0:T(2,128)(2,1)} %reshape.182), calls=%async_computation | async-start | bytes 1572864 | tf_op jit(solution)/shard_map/all_to_all | solution.py:263
  18.9 12.4 %all-to-all-done = bf16[16,2,12288]{2,1,0:T(2,128)(2,1)S(1)} async-done(((bf16[16,2,12288]{2,1,0:T(2,128)(2,1)}), bf16[16,2,12288]{2,1,0:T(2,128)(2,1)S(1)}, u32[]{:S(2)}, u32[]{:S(2)}) %all-to-all-start) | async-done | bytes 786464 | tf_op jit(solution)/shard_map/all_to_all | solution.py:263
  33.3 19.1 %shard_map.82 = (bf16[12,64,768]{2,1,0:T(8,128)(2,1)S(1)}, bf16[12,64,768]{2,1,0:T(8,128)(2,1)S(1)}) custom-call(bf16[12,4,48,4096]{3,2,1,0:T(8,128)(2,1)} %tile_ref.1, bf16[12,64,128]{2,1,0:T(8,128)(2,1)S(1)} %copy.55.coeff_ref), custom_call_target="tpu_custom_call" | custom-call | tf_op jit(solution)/shard_map/pallas_call | solution.py:126
  54.1 2.7 collective-permute-start.2
  56.7 22.0 %collective-permute-done.5.right_ref.far_b = bf16[12,64,768]{2,1,0:T(8,128)(2,1)} collective-permute-done((bf16[12,64,768]{2,1,0:T(8,128)(2,1)S(1)}, bf16[12,64,768]{2,1,0:T(8,128)(2,1)}, u32[]{:S(2)}, u32[]{:S(2)}) %collective-permute-start.5) | collective-permute-done | bytes 1179680 | tf_op jit(solution)/shard_map/ppermute | solution.py:301
  86.9 16.1 %collective-permute-done.2.left_ref.far_b = bf16[12,64,768]{2,1,0:T(8,128)(2,1)} collective-permute-done((bf16[12,64,768]{2,1,0:T(8,128)(2,1)S(1)}, bf16[12,64,768]{2,1,0:T(8,128)(2,1)}, u32[]{:S(2)}, u32[]{:S(2)}) %collective-permute-start.2) | collective-permute-done | bytes 1179680 | tf_op jit(solution)/shard_map/ppermute | solution.py:301
  103.0 2.6 collective-permute-start.3
  110.1 3.6 %shard_map.102 = bf16[12,64,768]{2,1,0:T(8,128)(2,1)S(1)} custom-call(s32[12]{0:T(128)S(1)} %pad_add_fusion.17.index_ref, bf16[12,64,768]{2,1,0:T(8,128)(2,1)} %collective-permute-done.10.far_b.left_ref, bf16[12,64,768]{2,1,0:T(8,128)(2,1)} %collective-permute-done.9.far_a.left_ref.right_ref), custom_call_target="tpu_custom_call" | custom-call | bytes 5242880 | tf_op jit(solution)/shard_map/pallas_call | solution.py:154
  114.3 15.8 %collective-permute-done.3.far_b.right_ref.left_ref = bf16[12,64,768]{2,1,0:T(8,128)(2,1)S(1)} collective-permute-done((bf16[12,64,768]{2,1,0:T(8,128)(2,1)}, bf16[12,64,768]{2,1,0:T(8,128)(2,1)S(1)}, u32[]{:S(2)}, u32[]{:S(2)}) %collective-permute-start.3) | collective-permute-done | bytes 1179680 | tf_op jit(solution)/shard_map/ppermute | solution.py:301
  130.1 2.7 shard_map.101
  134.9 20.5 %collective-permute-done.15.left_ref.right_ref.far_a = bf16[12,64,768]{2,1,0:T(8,128)(2,1)S(1)} collective-permute-done((bf16[12,64,768]{2,1,0:T(8,128)(2,1)}, bf16[12,64,768]{2,1,0:T(8,128)(2,1)S(1)}, u32[]{:S(2)}, u32[]{:S(2)}) %collective-permute-start.15) | collective-permute-done | bytes 1179680 | tf_op jit(solution)/shard_map/ppermute | solution.py:301
  159.4 2.7 shard_map.98
  172.3 12.1 %collective-permute-done.16.far_b.far_a = bf16[12,64,768]{2,1,0:T(8,128)(2,1)S(1)} collective-permute-done((bf16[12,64,768]{2,1,0:T(8,128)(2,1)S(1)}, bf16[12,64,768]{2,1,0:T(8,128)(2,1)S(1)}, u32[]{:S(2)}, u32[]{:S(2)}) %collective-permute-start.16) | collective-permute-done | bytes 1179680 | tf_op jit(solution)/shard_map/ppermute | solution.py:301
  203.8 3.6 %shard_map.84 = bf16[12,64,768]{2,1,0:T(8,128)(2,1)S(1)} custom-call(s32[12]{0:T(128)S(1)} %pad_add_fusion.3.index_ref, bf16[12,64,768]{2,1,0:T(8,128)(2,1)} %collective-permute-done.2.left_ref.far_b, bf16[12,64,768]{2,1,0:T(8,128)(2,1)} %collective-permute-done.5.right_ref.far_b), custom_call_target="tpu_custom_call" | custom-call | bytes 5242880 | tf_op jit(solution)/shard_map/pallas_call | solution.py:154
  207.5 3.8 %collective-permute-start.6 = (bf16[12,64,768]{2,1,0:T(8,128)(2,1)S(1)}, bf16[12,64,768]{2,1,0:T(8,128)(2,1)S(1)}, u32[]{:S(2)}, u32[]{:S(2)}) collective-permute-start(bf16[12,64,768]{2,1,0:T(8,128)(2,1)S(1)} %shard_map.84), channel_id=1, source_target_pairs={{0,24},{8,0},{16,8},{24,16},{32,56},{40,32},{48,40},{56,48},{64,88... | collective-permute-start | bytes 3538952 | tf_op jit(solution)/shard_map/ppermute | solution.py:301
  211.4 3.5 %shard_map.83 = bf16[12,64,768]{2,1,0:T(8,128)(2,1)S(1)} custom-call(s32[12]{0:T(128)S(1)} %pad_add_fusion.2.index_ref, bf16[12,64,768]{2,1,0:T(8,128)(2,1)} %collective-permute-done.left_ref.far_a, bf16[12,64,768]{2,1,0:T(8,128)(2,1)S(1)} %get-tuple-element.7.right_ref.c.far_a), custom_call_target="tpu_custom_call" | custom-call | bytes 5242880 | tf_op jit(solution)/shard_map/pallas_call | solution.py:154
  220.0 4.0 %collective-permute-done.11.far_a.far_b = bf16[12,64,768]{2,1,0:T(8,128)(2,1)S(1)} collective-permute-done((bf16[12,64,768]{2,1,0:T(8,128)(2,1)S(1)}, bf16[12,64,768]{2,1,0:T(8,128)(2,1)S(1)}, u32[]{:S(2)}, u32[]{:S(2)}) %collective-permute-start.11) | collective-permute-done | bytes 1179680 | tf_op jit(solution)/shard_map/ppermute | solution.py:301
  226.3 4.0 %shard_map.90._ = bf16[8,30,96,128]{3,2,1,0:T(8,128)(2,1)S(1)} custom-call(s32[12]{0:T(128)S(1)} %pad_add_fusion.8.index_ref, bf16[768,768]{1,0:T(8,128)(2,1)S(1)} %bitcast.39, bf16[768,768]{1,0:T(8,128)(2,1)S(1)} %bitcast.56, bf16[12,64,768]{2,1,0:T(8,128)(2,1)} %collective-permute-done.left_ref.far_a, ...), custom_call_target="tpu_custom_call", output_to_operand_aliasing={{}: (5, {})} | custom-call | flops 905969664 | bytes 6291456 | tf_op jit(solution)/shard_map/pallas_call | solution.py:199
  230.2 3.9 %shard_map.91._ = bf16[8,30,96,128]{3,2,1,0:T(8,128)(2,1)S(1)} custom-call(s32[12]{0:T(128)S(1)} %pad_add_fusion.7.index_ref, bf16[768,768]{1,0:T(8,128)(2,1)S(1)} %bitcast.40, bf16[768,768]{1,0:T(8,128)(2,1)S(1)} %bitcast.57, bf16[12,64,768]{2,1,0:T(8,128)(2,1)} %collective-permute-done.9.far_a.left_ref.right_ref, ...), custom_call_target="tpu_custom_call", output_to_operand_aliasing={{}: (5, {})} | custom-call | flops 905969664 | bytes 6291456 | tf_op jit(solution)/shard_map/pallas_call | solution.py:199
  238.7 3.5 %shard_map.94._ = bf16[8,30,96,128]{3,2,1,0:T(8,128)(2,1)S(1)} custom-call(s32[12]{0:T(128)S(1)} %get-tuple-element.44.index_ref, bf16[768,768]{1,0:T(8,128)(2,1)S(1)} %bitcast.43, bf16[768,768]{1,0:T(8,128)(2,1)S(1)} %bitcast.60, bf16[12,64,768]{2,1,0:T(8,128)(2,1)S(1)} %collective-permute-done.4.far_a, ...), custom_call_target="tpu_custom_call", output_to_operand_aliasing={{}: (5, {})} | custom-call | flops 905969664 | bytes 6291456 | tf_op jit(solution)/shard_map/pallas_call | solution.py:199
  244.6 3.5 %shard_map.96 = bf16[8,30,96,128]{3,2,1,0:T(8,128)(2,1)S(1)} custom-call(s32[12]{0:T(128)S(1)} %pad_add_fusion.1.index_ref, bf16[768,768]{1,0:T(8,128)(2,1)S(1)} %bitcast.45, bf16[768,768]{1,0:T(8,128)(2,1)S(1)} %bitcast.62, bf16[12,64,768]{2,1,0:T(8,128)(2,1)} %collective-permute-done.1.far_a.right_ref, ...), custom_call_target="tpu_custom_call", output_to_operand_aliasing={{}: (5, {})} | custom-call | flops 905969664 | bytes 6291456 | tf_op jit(solution)/shard_map/pallas_call | solution.py:199
  248.1 2.5 copy-done
  252.9 44.1 %reduce-scatter.3.cloned.1.call-done.first_ref = bf16[1,30,96,128]{3,2,1,0:T(8,128)(2,1)} async-done(((bf16[8,30,96,128]{3,2,1,0:T(8,128)(2,1)}), bf16[1,30,96,128]{3,2,1,0:T(8,128)(2,1)}) %reduce-scatter.3.cloned.1.call-update) | async-done | bytes 737296 | tf_op jit(solution)/shard_map/reduce_scatter | solution.py:323
  299.2 11.4 %shard_map.110 = bf16[96,12288]{1,0:T(8,128)(2,1)} custom-call(s32[192]{0:T(256)S(1)} %select_select_fusion.source_ref, s32[2]{0:T(128)S(1)} %pad_add_fusion.here_ref, bf16[1,30,96,128]{3,2,1,0:T(8,128)(2,1)S(1)} %copy-done.4, bf16[1,21,96,128]{3,2,1,0:T(8,128)(2,1)S(1)} %copy-done.5), custom_call_target="tpu_custom_call" | custom-call | tf_op jit(solution)/shard_map/pallas_call | solution.py:249
  (156 shorter events, 74.6 us)
Async XLA Ops:
  9.8 21.5 %all-to-all-start = ((bf16[16,2,12288]{2,1,0:T(2,128)(2,1)}), bf16[16,2,12288]{2,1,0:T(2,128)(2,1)S(1)}, u32[]{:S(2)}, u32[]{:S(2)}) async-start(bf16[16,2,12288]{2,1,0:T(2,128)(2,1)} %reshape.182), calls=%async_computation | async-start | bytes 1572864 | tf_op jit(solution)/shard_map/all_to_all | solution.py:263
  18.6 234.3 %reduce-scatter.5.cloned.1.call-start = ((), (), s32[]{:S(2)}) async-start(), calls=%async_computation.4 | async-start | bytes 4644864 | tf_op jit(solution)/shard_map/reduce_scatter | solution.py:323
  33.3 47.7 %copy-start.10 = (s32[192,4]{0,1:T(4,128)S(1)}, s32[192,4]{0,1:T(4,128)}, u32[]{:S(2)}) copy-start(s32[192,4]{0,1:T(4,128)} %param.11) | copy-start | bytes 9220
  52.4 26.3 %collective-permute-start.5 = (bf16[12,64,768]{2,1,0:T(8,128)(2,1)S(1)}, bf16[12,64,768]{2,1,0:T(8,128)(2,1)}, u32[]{:S(2)}, u32[]{:S(2)}) collective-permute-start(bf16[12,64,768]{2,1,0:T(8,128)(2,1)S(1)} %get-tuple-element.8.left_ref.d.far_b), channel_id=1, source_target_pairs={{0,32},{8,40},{16,48},{24,56},{32,64},{40,72},{48,80},{56,88},{64,... | collective-permute-start | bytes 3538952 | tf_op jit(solution)/shard_map/ppermute | solution.py:301
  52.5 26.6 %collective-permute-start = (bf16[12,64,768]{2,1,0:T(8,128)(2,1)S(1)}, bf16[12,64,768]{2,1,0:T(8,128)(2,1)}, u32[]{:S(2)}, u32[]{:S(2)}) collective-permute-start(bf16[12,64,768]{2,1,0:T(8,128)(2,1)S(1)} %get-tuple-element.7.right_ref.c.far_a), channel_id=1, source_target_pairs={{0,24},{8,0},{16,8},{24,16},{32,56},{40,32},{48,40},{56,48},{64,88... | collective-permute-start | bytes 3538952 | tf_op jit(solution)/shard_map/ppermute | solution.py:301
  54.1 26.9 %collective-permute-start.7 = (bf16[12,64,768]{2,1,0:T(8,128)(2,1)S(1)}, bf16[12,64,768]{2,1,0:T(8,128)(2,1)S(1)}, u32[]{:S(2)}, u32[]{:S(2)}) collective-permute-start(bf16[12,64,768]{2,1,0:T(8,128)(2,1)S(1)} %get-tuple-element.7.right_ref.c.far_a), channel_id=1, source_target_pairs={{0,8},{8,16},{16,24},{24,0},{32,40},{40,48},{48,56},{56,32},{64,72... | collective-permute-start | bytes 3538952 | tf_op jit(solution)/shard_map/ppermute | solution.py:301
  54.1 48.9 %collective-permute-start.2 = (bf16[12,64,768]{2,1,0:T(8,128)(2,1)S(1)}, bf16[12,64,768]{2,1,0:T(8,128)(2,1)}, u32[]{:S(2)}, u32[]{:S(2)}) collective-permute-start(bf16[12,64,768]{2,1,0:T(8,128)(2,1)S(1)} %get-tuple-element.8.left_ref.d.far_b), channel_id=1, source_target_pairs={{0,24},{8,0},{16,8},{24,16},{32,56},{40,32},{48,40},{56,48},{64,88... | collective-permute-start | bytes 3538952 | tf_op jit(solution)/shard_map/ppermute | solution.py:301
  78.7 26.9 %collective-permute-start.10 = (bf16[12,64,768]{2,1,0:T(8,128)(2,1)}, bf16[12,64,768]{2,1,0:T(8,128)(2,1)}, u32[]{:S(2)}, u32[]{:S(2)}) collective-permute-start(bf16[12,64,768]{2,1,0:T(8,128)(2,1)} %collective-permute-done.5.right_ref.far_b), channel_id=1, source_target_pairs={{0,8},{8,16},{16,24},{24,0},{32,40},{40,48},{48,56},{56,32},{64,72... | collective-permute-start | bytes 3538952 | tf_op jit(solution)/shard_map/ppermute | solution.py:301
  79.1 27.7 %collective-permute-start.1 = (bf16[12,64,768]{2,1,0:T(8,128)(2,1)}, bf16[12,64,768]{2,1,0:T(8,128)(2,1)}, u32[]{:S(2)}, u32[]{:S(2)}) collective-permute-start(bf16[12,64,768]{2,1,0:T(8,128)(2,1)} %collective-permute-done.left_ref.far_a), channel_id=1, source_target_pairs={{0,96},{8,104},{16,112},{24,120},{32,0},{40,8},{48,16},{56,24},{64... | collective-permute-start | bytes 3538952 | tf_op jit(solution)/shard_map/ppermute | solution.py:301
  81.0 29.1 %collective-permute-start.9 = (bf16[12,64,768]{2,1,0:T(8,128)(2,1)S(1)}, bf16[12,64,768]{2,1,0:T(8,128)(2,1)}, u32[]{:S(2)}, u32[]{:S(2)}) collective-permute-start(bf16[12,64,768]{2,1,0:T(8,128)(2,1)S(1)} %collective-permute-done.7.right_ref.far_a.left_ref), channel_id=1, source_target_pairs={{0,32},{8,40},{16,48},{24,56},{32,64},{40,72},{48,80},{56,88},{64,... | collective-permute-start | bytes 3538952 | tf_op jit(solution)/shard_map/ppermute | solution.py:301
  103.0 27.1 %collective-permute-start.3 = (bf16[12,64,768]{2,1,0:T(8,128)(2,1)}, bf16[12,64,768]{2,1,0:T(8,128)(2,1)S(1)}, u32[]{:S(2)}, u32[]{:S(2)}) collective-permute-start(bf16[12,64,768]{2,1,0:T(8,128)(2,1)} %collective-permute-done.2.left_ref.far_b), channel_id=1, source_target_pairs={{0,96},{8,104},{16,112},{24,120},{32,0},{40,8},{48,16},{56,24},{64... | collective-permute-start | bytes 3538952 | tf_op jit(solution)/shard_map/ppermute | solution.py:301
  105.7 29.3 %collective-permute-start.13 = (bf16[12,64,768]{2,1,0:T(8,128)(2,1)}, bf16[12,64,768]{2,1,0:T(8,128)(2,1)S(1)}, u32[]{:S(2)}, u32[]{:S(2)}) collective-permute-start(bf16[12,64,768]{2,1,0:T(8,128)(2,1)} %collective-permute-done.10.far_b.left_ref), channel_id=1, source_target_pairs={{0,32},{8,40},{16,48},{24,56},{32,64},{40,72},{48,80},{56,88},{64,... | collective-permute-start | bytes 3538952 | tf_op jit(solution)/shard_map/ppermute | solution.py:301
  106.8 48.6 %collective-permute-start.15 = (bf16[12,64,768]{2,1,0:T(8,128)(2,1)}, bf16[12,64,768]{2,1,0:T(8,128)(2,1)S(1)}, u32[]{:S(2)}, u32[]{:S(2)}) collective-permute-start(bf16[12,64,768]{2,1,0:T(8,128)(2,1)} %collective-permute-done.1.far_a.right_ref), channel_id=1, source_target_pairs={{0,96},{8,104},{16,112},{24,120},{32,0},{40,8},{48,16},{56,24},{64... | collective-permute-start | bytes 3538952 | tf_op jit(solution)/shard_map/ppermute | solution.py:301
  113.7 51.0 %collective-permute-start.19 = (bf16[12,64,768]{2,1,0:T(8,128)(2,1)S(1)}, bf16[12,64,768]{2,1,0:T(8,128)(2,1)S(1)}, u32[]{:S(2)}, u32[]{:S(2)}) collective-permute-start(bf16[12,64,768]{2,1,0:T(8,128)(2,1)S(1)} %shard_map.102), channel_id=1, source_target_pairs={{0,8},{8,16},{16,24},{24,0},{32,40},{40,48},{48,56},{56,32},{64,72... | collective-permute-start | bytes 3538952 | tf_op jit(solution)/shard_map/ppermute | solution.py:301
  132.8 37.2 %collective-permute-start.18 = (bf16[12,64,768]{2,1,0:T(8,128)(2,1)S(1)}, bf16[12,64,768]{2,1,0:T(8,128)(2,1)S(1)}, u32[]{:S(2)}, u32[]{:S(2)}) collective-permute-start(bf16[12,64,768]{2,1,0:T(8,128)(2,1)S(1)} %shard_map.101), channel_id=1, source_target_pairs={{0,24},{8,0},{16,8},{24,16},{32,56},{40,32},{48,40},{56,48},{64,88... | collective-permute-start | bytes 3538952 | tf_op jit(solution)/shard_map/ppermute | solution.py:301
  156.3 28.1 %collective-permute-start.16 = (bf16[12,64,768]{2,1,0:T(8,128)(2,1)S(1)}, bf16[12,64,768]{2,1,0:T(8,128)(2,1)S(1)}, u32[]{:S(2)}, u32[]{:S(2)}) collective-permute-start(bf16[12,64,768]{2,1,0:T(8,128)(2,1)S(1)} %shard_map.99), channel_id=1, source_target_pairs={{0,24},{8,0},{16,8},{24,16},{32,56},{40,32},{48,40},{56,48},{64,88... | collective-permute-start | bytes 3538952 | tf_op jit(solution)/shard_map/ppermute | solution.py:301
  159.2 25.2 %collective-permute-start.17 = (bf16[12,64,768]{2,1,0:T(8,128)(2,1)S(1)}, bf16[12,64,768]{2,1,0:T(8,128)(2,1)S(1)}, u32[]{:S(2)}, u32[]{:S(2)}) collective-permute-start(bf16[12,64,768]{2,1,0:T(8,128)(2,1)S(1)} %shard_map.100), channel_id=1, source_target_pairs={{0,8},{8,16},{16,24},{24,0},{32,40},{40,48},{48,56},{56,32},{64,72... | collective-permute-start | bytes 3538952 | tf_op jit(solution)/shard_map/ppermute | solution.py:301
  162.1 25.9 %collective-permute-start.14 = (bf16[12,64,768]{2,1,0:T(8,128)(2,1)S(1)}, bf16[12,64,768]{2,1,0:T(8,128)(2,1)S(1)}, u32[]{:S(2)}, u32[]{:S(2)}) collective-permute-start(bf16[12,64,768]{2,1,0:T(8,128)(2,1)S(1)} %shard_map.98), channel_id=1, source_target_pairs={{0,32},{8,40},{16,48},{24,56},{32,64},{40,72},{48,80},{56,88},{64,... | collective-permute-start | bytes 3538952 | tf_op jit(solution)/shard_map/ppermute | solution.py:301
  164.7 27.9 %collective-permute-start.12 = (bf16[12,64,768]{2,1,0:T(8,128)(2,1)S(1)}, bf16[12,64,768]{2,1,0:T(8,128)(2,1)S(1)}, u32[]{:S(2)}, u32[]{:S(2)}) collective-permute-start(bf16[12,64,768]{2,1,0:T(8,128)(2,1)S(1)} %shard_map.97), channel_id=1, source_target_pairs={{0,96},{8,104},{16,112},{24,120},{32,0},{40,8},{48,16},{56,24},{64... | collective-permute-start | bytes 3538952 | tf_op jit(solution)/shard_map/ppermute | solution.py:301
  199.1 97.9 %reduce-scatter.3.cloned.1.call-start = ((), (), s32[]{:S(2)}) async-start(), calls=%async_computation.3 | async-start | bytes 6635520 | tf_op jit(solution)/shard_map/reduce_scatter | solution.py:323
  200.8 23.2 %collective-permute-start.11 = (bf16[12,64,768]{2,1,0:T(8,128)(2,1)S(1)}, bf16[12,64,768]{2,1,0:T(8,128)(2,1)S(1)}, u32[]{:S(2)}, u32[]{:S(2)}) collective-permute-start(bf16[12,64,768]{2,1,0:T(8,128)(2,1)S(1)} %shard_map.86), channel_id=1, source_target_pairs={{0,96},{8,104},{16,112},{24,120},{32,0},{40,8},{48,16},{56,24},{64... | collective-permute-start | bytes 3538952 | tf_op jit(solution)/shard_map/ppermute | solution.py:301
  203.7 30.5 %collective-permute-start.8 = (bf16[12,64,768]{2,1,0:T(8,128)(2,1)S(1)}, bf16[12,64,768]{2,1,0:T(8,128)(2,1)S(1)}, u32[]{:S(2)}, u32[]{:S(2)}) collective-permute-start(bf16[12,64,768]{2,1,0:T(8,128)(2,1)S(1)} %shard_map.85), channel_id=1, source_target_pairs={{0,8},{8,16},{16,24},{24,0},{32,40},{40,48},{48,56},{56,32},{64,72... | collective-permute-start | bytes 3538952 | tf_op jit(solution)/shard_map/ppermute | solution.py:301
  207.5 29.0 %collective-permute-start.6 = (bf16[12,64,768]{2,1,0:T(8,128)(2,1)S(1)}, bf16[12,64,768]{2,1,0:T(8,128)(2,1)S(1)}, u32[]{:S(2)}, u32[]{:S(2)}) collective-permute-start(bf16[12,64,768]{2,1,0:T(8,128)(2,1)S(1)} %shard_map.84), channel_id=1, source_target_pairs={{0,24},{8,0},{16,8},{24,16},{32,56},{40,32},{48,40},{56,48},{64,88... | collective-permute-start | bytes 3538952 | tf_op jit(solution)/shard_map/ppermute | solution.py:301
  214.9 23.8 %collective-permute-start.4 = (bf16[12,64,768]{2,1,0:T(8,128)(2,1)S(1)}, bf16[12,64,768]{2,1,0:T(8,128)(2,1)S(1)}, u32[]{:S(2)}, u32[]{:S(2)}) collective-permute-start(bf16[12,64,768]{2,1,0:T(8,128)(2,1)S(1)} %shard_map.83), channel_id=1, source_target_pairs={{0,32},{8,40},{16,48},{24,56},{32,64},{40,72},{48,80},{56,88},{64,... | collective-permute-start | bytes 3538952 | tf_op jit(solution)/shard_map/ppermute | solution.py:301
  (21 other events, 114.3 us)
Sparse Core Ops, SparseCore 0:
  199.2 38.6 reduce-scatter.4
  250.8 46.1 reduce-scatter.2

commit v2 on v0

v2 whole, which is shorter than its diff:
```python
import functools
import math

import jax
import jax.numpy as jnp
import numpy as np
from jax import lax
from jax.experimental import pallas as pl
from jax.experimental.pallas import tpu as pltpu
from jax.sharding import PartitionSpec as P

BS = 64
KB = 4
NBD = 12
CAP = 6
NP = 48
GAP = 56
NOCC = 32
HALF = NP * NOCC // 2
SIDE = 4
FIT = 8
ROWS = NBD * BS
PIECE = ROWS // FIT
MIB = 2**20

STEP = {"+y": (1, 0), "-y": (3, 0), "+z": (0, 1), "-z": (0, 3)}
NEAR = tuple(STEP.values())
MIDDLE = ((2, 0), (0, 2))
FAR = (((2, 2), (2, 0)), ((2, 2), (0, 2)))
CORNERS = (((1, 3), (0, 3)), ((3, 1), (0, 1)), ((1, 1), (1, 0)), ((3, 3), (3, 0)))
EDGES = (((2, 1), (2, 0)), ((2, 3), (2, 0)), ((1, 2), (0, 2)), ((3, 2), (0, 2)))
LEAVES = CORNERS + EDGES + FAR
CHUNKS = (
    NEAR,
    MIDDLE + tuple(o for o, _ in CORNERS),
    tuple(o for o, _ in EDGES) + ((2, 2),),
)
TILES = CAP // 2
OWN_TILES = NBD // 2
BASE = {(0, 0): 0}
for _o in sum(CHUNKS, ()):
    BASE[_o] = OWN_TILES + TILES * (len(BASE) - 1)
COUNT = tuple(TILES * len(c) + (OWN_TILES if n == 0 else 0) for n, c in enumerate(CHUNKS))
TOTAL = sum(COUNT)


def minus(a, b):
    return ((a[0] - b[0]) % SIDE, (a[1] - b[1]) % SIDE)


def plus(a, b):
    return ((a[0] + b[0]) % SIDE, (a[1] + b[1]) % SIDE)


def number(a):
    return a[0] * SIDE + a[1]


PLACES = tuple((y, z) for y in range(SIDE) for z in range(SIDE))
WHOLE = NEAR + MIDDLE
PAIRS = np.array(
    [
        [(number(minus(me, o)), number(me)) for o in WHOLE]
        + [
            (number(minus(me, sender)), number(plus(me, minus(o, sender))))
            for o, sender in LEAVES
        ]
        for me in PLACES
    ],
    dtype=np.int32,
)
BASE_OF = np.array([[BASE[minus(me, h)] for h in PLACES] for me in PLACES], dtype=np.int32)


def fit_kernel(tile_ref, coeff_ref, out_ref, lines):
    for m in range(2):
        for k in range(KB):
            for pair in range(BS // 2):
                value = tile_ref[m, k, :, pair * 128 : (pair + 1) * 128]
                lines[m, pl.ds((k * 32 + pair) * GAP, NP), :] = value.astype(jnp.float32)
    for group in range(NP // 4):
        both = []
        for m in range(2):
            parts = []
            for p in range(group * 4, group * 4 + 4):
                rows = lines[m, pl.ds(p, 128, stride=GAP), :].astype(jnp.bfloat16)
                product = jnp.dot(coeff_ref[m], rows, preferred_element_type=jnp.float32)
                parts.append(product[0:NOCC] + pltpu.roll(product[NOCC:], 64, 1))
            both.append(jnp.concatenate(parts, axis=0)[:, 0:BS])
        turned = jnp.concatenate(both, axis=1).T.astype(jnp.bfloat16)
        place = (group % 6) * 128
        out_ref[group // 6, 0, :, place : place + 128] = turned[0:BS]
        out_ref[group // 6, 1, :, place : place + 128] = turned[BS:]


def fit_rows(three_centre, picked):
    return pl.pallas_call(
        fit_kernel,
        grid=(NBD // 2,),
        in_specs=[
            pl.BlockSpec((2, KB, NP, BS * BS), lambda g: (g, 0, 0, 0)),
            pl.BlockSpec((2, 2 * NOCC, 128), lambda g: (g, 0, 0)),
        ],
        out_specs=pl.BlockSpec((2, 2, BS, HALF), lambda g: (0, g, 0, 0)),
        out_shape=jax.ShapeDtypeStruct((2, NBD, BS, HALF), jnp.bfloat16),
        scratch_shapes=[pltpu.VMEM((2, KB * 32 * GAP, 128), jnp.float32)],
        compiler_params=pltpu.CompilerParams(vmem_limit_bytes=58 * MIB),
    )(three_centre, picked)


def pack_kernel(jobs, n_in, index_ref, *refs):
    ins, outs, sems = refs[:n_in], refs[n_in:-1], refs[-1]
    copies = []
    for out, parts in zip(outs, jobs, strict=True):
        at = 0
        for source, row, first in parts:
            if row is None:
                copies.append((ins[source].at[pl.ds(first, NBD)], out.at[pl.ds(at, NBD)]))
                at += NBD
                continue
            for s in range(CAP):
                copies.append((ins[source].at[first + index_ref[row, s]], out.at[at + s]))
            at += CAP
    copies = [pltpu.make_async_copy(*copy, sems.at[n]) for n, copy in enumerate(copies)]
    for copy in copies:
        copy.start()
    for copy in copies:
        copy.wait()


def pack(jobs, sources, index, after):
    count = [sum(NBD if row is None else CAP for _, row, _ in parts) for parts in jobs]
    copies = sum(1 if row is None else CAP for parts in jobs for _, row, _ in parts)
    operands = [*sources, *after]
    return pl.pallas_call(
        functools.partial(pack_kernel, jobs, len(operands)),
        in_specs=[pl.BlockSpec(memory_space=pltpu.SMEM)]
        + [pl.BlockSpec(memory_space=pl.ANY)] * len(operands),
        out_specs=[pl.BlockSpec(memory_space=pltpu.VMEM)] * len(jobs),
        out_shape=[jax.ShapeDtypeStruct((n, BS, HALF), jnp.bfloat16) for n in count],
        scratch_shapes=[pltpu.SemaphoreType.DMA((copies,))],
        compiler_params=pltpu.CompilerParams(vmem_limit_bytes=58 * MIB),
        cost_estimate=pl.CostEstimate(flops=0, bytes_accessed=MIB, transcendentals=0),
    )(index, *operands)


def product_kernel(scale, jobs, n_in, split, index_ref, here_ref, own_ref, *refs):
    ins, outs = refs[:n_in], refs[n_in:-4]
    left, side, own_sems, sems = refs[-4:]
    step = pl.program_id(0)
    core = here_ref[1] & 1

    def own_copies():
        made = []
        for half in range(2):
            for n in range(FIT):
                piece = n
                if split:
                    piece = 2 * (n % (FIT // 2)) + (core if n < FIT // 2 else 1 - core)
                given = own_ref.at[half, pl.ds(pl.multiple_of(piece * PIECE, 32), PIECE)]
                made.append((given, left.at[half, pl.ds(n * PIECE, PIECE)], own_sems.at[half, n]))
        return [pltpu.make_async_copy(*copy) for copy in made]

    def copies(job, slot):
        made = []
        for half, (source, row, first) in enumerate(jobs[job]):
            if row is None:
                given = ins[source].at[pl.ds(first, CAP)]
                made.append((given, side.at[slot, half], sems.at[slot, half, 0]))
                continue
            for s in range(CAP):
                given = ins[source].at[first + index_ref[row, s]]
                made.append((given, side.at[slot, half, s], sems.at[slot, half, s]))
        return [pltpu.make_async_copy(*copy) for copy in made]

    def begin(job):
        for copy in copies(job, job % 2):
            copy.start()

    @pl.when(step == 0)
    def _():
        for copy in own_copies():
            copy.start()
        begin(0)
        for copy in own_copies():
            copy.wait()

    for job in range(len(jobs)):

        @pl.when(step == job)
        def _(job=job):
            if job + 1 < len(jobs):
                begin(job + 1)
            for copy in copies(job, job % 2):
                copy.wait()

    slot = lax.rem(step, 2)
    last = (((1,), (1,)), ((), ()))
    side_a = side[slot, 0].reshape(CAP * BS, HALF)
    side_b = side[slot, 1].reshape(CAP * BS, HALF)
    total = lax.dot_general(left[0], side_a, last, preferred_element_type=jnp.float32)
    total += lax.dot_general(left[1], side_b, last, preferred_element_type=jnp.float32)
    total = (total * scale).astype(jnp.bfloat16)
    pieces = FIT // len(outs)
    for n in range(FIT):
        for t in range(TILES):
            part = total[n * PIECE : (n + 1) * PIECE, t * 128 : (t + 1) * 128]
            outs[n // pieces][n % pieces, t] = part


def product(
    own, jobs, sources, index, here, buffers, tile, count, scale, after, split, cost
):
    anywhere = pl.BlockSpec(memory_space=pl.ANY)
    smem = pl.BlockSpec(memory_space=pltpu.SMEM)
    extra = list(after) + list(buffers)
    given = [own.reshape(2, ROWS, HALF), *sources, *extra]
    operands = [index, here, *given]
    pieces = FIT // 2 if split else FIT
    shape = (pieces, count, PIECE, 128)
    kinds = [jnp.bfloat16] * (2 if split else 1)
    out = pl.BlockSpec((pieces, TILES, PIECE, 128), lambda j: (0, tile // TILES + j, 0, 0))
    return pl.pallas_call(
        functools.partial(product_kernel, scale, jobs, len(sources) + len(extra), split),
        grid=(len(jobs),),
        in_specs=[smem, smem] + [anywhere] * len(given),
        out_specs=[out] * len(kinds),
        out_shape=[jax.ShapeDtypeStruct(shape, kind) for kind in kinds],
        scratch_shapes=[
            pltpu.VMEM((2, ROWS, HALF), jnp.bfloat16),
            pltpu.VMEM((2, 2, CAP, BS, HALF), jnp.bfloat16),
            pltpu.SemaphoreType.DMA((2, FIT)),
            pltpu.SemaphoreType.DMA((2, 2, CAP)),
        ],
        input_output_aliases={len(operands) - len(buffers) + n: n for n in range(len(buffers))},
        compiler_params=pltpu.CompilerParams(vmem_limit_bytes=58 * MIB),
        cost_estimate=pl.CostEstimate(flops=cost, bytes_accessed=MIB, transcendentals=0),
    )(*operands)


def add_kernel(here_ref, keep_ref, came_ref, own_ref, *send_refs):
    x = here_ref[1] >> 1
    own_ref[...] = keep_ref[x].astype(jnp.float32) + came_ref[x].astype(jnp.float32)
    for shift, send_ref in zip((1, 2, 3), send_refs, strict=True):
        there = (x + shift) & (SIDE - 1)
        value = keep_ref[there].astype(jnp.float32) + came_ref[there].astype(jnp.float32)
        send_ref[...] = value.astype(jnp.bfloat16)


def add_all_kernel(keep_ref, came_ref, out_ref):
    total = keep_ref[...].astype(jnp.float32) + came_ref[...].astype(jnp.float32)
    out_ref[...] = total.astype(jnp.bfloat16)


def add_cores_all(keep, came):
    block = pl.BlockSpec((FIT // 2, TILES, PIECE, 128), lambda j: (0, j, 0, 0))
    return pl.pallas_call(
        add_all_kernel,
        grid=(keep.shape[1] // TILES,),
        in_specs=[block, block],
        out_specs=block,
        out_shape=jax.ShapeDtypeStruct(keep.shape, jnp.bfloat16),
        compiler_params=pltpu.CompilerParams(vmem_limit_bytes=58 * MIB),
        cost_estimate=pl.CostEstimate(flops=0, bytes_accessed=MIB, transcendentals=0),
    )(keep, came)


def add_cores(here, keep, came):
    count = keep.shape[1]
    block = pl.BlockSpec((FIT // 2, TILES, PIECE, 128), lambda j: (0, j, 0, 0))
    out = pl.BlockSpec((TILES, PIECE, 128), lambda j: (j, 0, 0))
    shape = (count, PIECE, 128)
    return pl.pallas_call(
        add_kernel,
        grid=(count // TILES,),
        in_specs=[pl.BlockSpec(memory_space=pltpu.SMEM), block, block],
        out_specs=[out] * 4,
        out_shape=[jax.ShapeDtypeStruct(shape, jnp.float32)]
        + [jax.ShapeDtypeStruct(shape, jnp.bfloat16)] * 3,
        compiler_params=pltpu.CompilerParams(vmem_limit_bytes=58 * MIB),
        cost_estimate=pl.CostEstimate(flops=0, bytes_accessed=MIB, transcendentals=0),
    )(here, keep, came)


def sum_kernel(given_ref, out_ref):
    value = given_ref[0].astype(jnp.float32)
    for n in range(1, given_ref.shape[0]):
        value += given_ref[n].astype(jnp.float32)
    out_ref[0] = value.astype(jnp.bfloat16)
    for t in range(TILES):
        out_ref[1, t] = pltpu.roll(value[t], 64, 1).astype(jnp.bfloat16)


def sum_pieces(given):
    count = given.shape[1]
    return pl.pallas_call(
        sum_kernel,
        grid=(count // TILES,),
        in_specs=[pl.BlockSpec((given.shape[0], TILES, PIECE, 128), lambda j: (0, j, 0, 0))],
        out_specs=pl.BlockSpec((2, TILES, PIECE, 128), lambda j: (0, j, 0, 0)),
        out_shape=jax.ShapeDtypeStruct((2, count, PIECE, 128), jnp.bfloat16),
        compiler_params=pltpu.CompilerParams(vmem_limit_bytes=58 * MIB),
        cost_estimate=pl.CostEstimate(flops=0, bytes_accessed=MIB, transcendentals=0),
    )(given)


def place_kernel(left_ref, right_ref, here_ref, *refs):
    parts, (out_ref, own, came, tiles, sems) = refs[:-5], refs[-5:]
    copies = []
    begin = 0
    for n, count in enumerate(COUNT[:2]):
        for turned in range(2):
            to = tiles.at[pl.ds(turned * (TOTAL + 1) + begin, count)]
            copies.append((parts[n].at[turned], to, sems.at[len(copies)]))
        begin += count
    copies.append((parts[2], own, sems.at[4]))
    copies += [(parts[3 + m], came.at[m], sems.at[5 + m]) for m in range(3)]
    copies = [pltpu.make_async_copy(*copy) for copy in copies]
    for copy in copies:
        copy.start()
    tiles[TOTAL] = jnp.zeros((PIECE, 128), jnp.bfloat16)
    for copy in copies:
        copy.wait()

    def add(tile, _):
        value = own[tile]
        for m in range(3):
            value += came[m, tile].astype(jnp.float32)
        tiles[begin + tile] = value.astype(jnp.bfloat16)
        tiles[TOTAL + 1 + begin + tile] = pltpu.roll(value, 64, 1).astype(jnp.bfloat16)
        return 0

    lax.fori_loop(0, COUNT[2], add, 0, unroll=3)
    is_left = lax.broadcasted_iota(jnp.int32, (PIECE, 128), 1) < 64

    def one(pair, _):
        value = jnp.where(is_left, tiles[left_ref[pair]], tiles[right_ref[pair]])
        out_ref[:, pl.ds(pl.multiple_of(pair * 128, 128), 128)] = value
        return 0

    lax.fori_loop(0, SIDE * SIDE * NBD // 2, one, 0, unroll=4)
    lane = lax.broadcasted_iota(jnp.int32, (PIECE, 128), 1)
    line = lax.broadcasted_iota(jnp.int32, (PIECE, 128), 0)
    row_block = (line + here_ref[1] * PIECE) >> 6
    for pair in range(NBD // 2):
        at = pl.ds(pl.multiple_of((here_ref[0] * (NBD // 2) + pair) * 128, 128), 128)
        value = out_ref[:, at].astype(jnp.float32)
        value = jnp.where(row_block == 2 * pair + (lane >> 6), 0.0, value)
        out_ref[:, at] = value.astype(jnp.bfloat16)


def place(source, here, parts):
    tile, odd = source >> 1, source & 1
    left = jnp.where(source < 0, TOTAL, jnp.where(odd == 0, tile, tile + TOTAL + 1))[0::2]
    right = jnp.where(source < 0, TOTAL, jnp.where(odd == 1, tile, tile + TOTAL + 1))[1::2]
    smem = pl.BlockSpec(memory_space=pltpu.SMEM)
    return pl.pallas_call(
        place_kernel,
        in_specs=[smem, smem, smem] + [pl.BlockSpec(memory_space=pl.ANY)] * len(parts),
        out_specs=pl.BlockSpec(memory_space=pltpu.VMEM),
        out_shape=jax.ShapeDtypeStruct((PIECE, SIDE * SIDE * NBD * BS), jnp.bfloat16),
        scratch_shapes=[
            pltpu.VMEM((COUNT[2], PIECE, 128), jnp.float32),
            pltpu.VMEM((3, COUNT[2], PIECE, 128), jnp.bfloat16),
            pltpu.VMEM((2 * TOTAL + 1, PIECE, 128), jnp.bfloat16),
            pltpu.SemaphoreType.DMA((8,)),
        ],
        compiler_params=pltpu.CompilerParams(vmem_limit_bytes=58 * MIB),
    )(left, right, here, *parts)


def per_device(three_centre, tensor_pattern, coefficients, readers):
    groups = SIDE * SIDE
    me = lax.axis_index("atom")
    lane = lax.axis_index("fit")
    mine = coefficients.reshape(NOCC, NBD, 32, 2).transpose(1, 3, 0, 2).reshape(NBD, 2 * NOCC, 32)
    everyone = lax.all_to_all(
        jnp.broadcast_to(mine[None], (groups,) + mine.shape), "atom", 0, 0, tiled=True
    ).reshape(groups * NBD, 2 * NOCC, 32)
    picked = jnp.take(everyone, tensor_pattern.reshape(-1), axis=0)
    picked = picked.reshape(NBD, KB, 2 * NOCC, 32).transpose(0, 2, 1, 3).reshape(NBD, 2 * NOCC, 128)
    own = fit_rows(three_centre, picked)

    by_group = readers.reshape(groups, NBD, 4)
    pairs = jnp.asarray(PAIRS)[me]
    hit = jnp.any(by_group[pairs[:, 0]] == pairs[:, 1][:, None, None], axis=2)
    numbers = jnp.arange(NBD, dtype=jnp.int32)
    earlier = numbers[:, None] < numbers[None, :]
    rank = jnp.sum((hit[:, :, None] & earlier[None]).astype(jnp.int32), axis=1)
    slots = jnp.arange(CAP, dtype=jnp.int32)
    chosen = hit[:, None, :] & (rank[:, None, :] == slots[None, :, None])
    lists = jnp.sum(chosen.astype(jnp.int32) * numbers[None, None, :], axis=2)
    reads = jnp.any(by_group == me, axis=2)
    read_rank = jnp.sum((reads[:, :, None] & earlier[None]).astype(jnp.int32), axis=1)
    source = jnp.where(reads, 2 * jnp.asarray(BASE_OF)[me][:, None] + read_rank, -1)
    source = jnp.where(jnp.arange(groups)[:, None] == me, numbers[None, :], source).reshape(-1)

    scale = 1.0 / math.sqrt(FIT * 2 * HALF)
    def send(payload, step):
        route = [(number(a), number(plus(a, step))) for a in PLACES]
        return lax.ppermute(payload, "atom", route)

    here = jnp.stack([me, lane]).astype(jnp.int32)

    def multiply(jobs, buffers, tile, count, after, split=False, cost=0):
        sources = []
        for pair in jobs:
            for array, _, _ in pair:
                if not any(array is known for known in sources):
                    sources.append(array)
        at = lambda array: next(n for n, known in enumerate(sources) if known is array)
        jobs = tuple(tuple((at(array), row, first) for array, row, first in p) for p in jobs)
        return product(
            own, jobs, sources, lists, here, buffers, tile, count, scale, after, split, cost
        )

    def over_cores(to_send):
        return lax.ppermute(to_send, "fit", [(n, n ^ 1) for n in range(FIT)])

    def over_chips(pieces):
        sent = []
        for shift, piece in zip((1, 2, 3), pieces, strict=True):
            route = [(n, (n + 2 * shift) % FIT) for n in range(FIT)]
            sent.append(lax.ppermute(piece, "fit", route))
        return sent

    def exchange(pieces):
        groups = [list(range(core, FIT, 2)) for core in range(2)]
        return lax.all_to_all(pieces, "fit", 0, 0, axis_index_groups=groups, tiled=True)

    def leaf_row(o):
        return len(WHOLE) + [p[0] for p in LEAVES].index(o)

    def both(source, row):
        return ((source, row, 0), (source, row, NBD))

    def hop(leaf):
        return minus(*leaf)

    own = own.reshape(2 * NBD, BS, HALF)
    near = [send(own, o) for o in NEAR]
    jobs = [[(own, None, half * NBD + part * CAP) for half in range(2)] for part in range(2)]
    partial = multiply(jobs, [], 0, COUNT[0], [], True)
    jobs = []
    for n, (o, sender) in enumerate(CORNERS):
        jobs.append(((n, None, (n % 2) * NBD), *both(NEAR.index(sender), leaf_row(o))))
    packed = pack(tuple(jobs), near, lists, partial[:1])
    second = [send(packed[n], o) for n, o in enumerate(NEAR)]
    jobs = [[(near[n], n, 0), (near[n], n, NBD)] for n in range(4)]
    keep, to_send = multiply(jobs, partial, OWN_TILES, COUNT[0], packed[:1], True)
    first_pieces = add_cores_all(keep, over_cores(to_send))
    jobs = []
    for o, sender in EDGES:
        m, row = 2 * MIDDLE.index(sender), leaf_row(o)
        jobs.append(((m, row, 0), (m + 1, row, 0)))
    jobs.append(((0, leaf_row((2, 2)), 0),))
    packed = pack(tuple(jobs), second, lists, [first_pieces])
    last = [send(packed[4], hop(FAR[0]))]
    third = [send(packed[n], hop(leaf)) for n, leaf in enumerate(EDGES)]
    first_came = exchange(first_pieces)
    jobs = [[(second[2 * m], 4 + m, 0), (second[2 * m + 1], 4 + m, 0)] for m in range(2)]
    jobs += [[(second[n], None, NBD), (second[n], None, NBD + CAP)] for n in range(4)]
    (partial,) = multiply(jobs, [], 0, COUNT[1], packed[:1])
    second_came = lax.all_to_all(partial, "fit", 0, 0, tiled=True)
    jobs = (((0, leaf_row((2, 2)) + 1, 0),),)
    last.append(send(pack(jobs, second[3:], lists, [partial])[0], hop(FAR[1])))
    jobs = [[(array, None, 0), (array, None, CAP)] for array in third]
    jobs.append([(array, None, 0) for array in last])
    keep, to_send = multiply(jobs, [], 0, COUNT[2], [first_came], True, 10**12)
    pieces = add_cores(here, keep, over_cores(to_send))
    third_came = over_chips(pieces[1:])
    parts = [sum_pieces(first_came), sum_pieces(second_came), pieces[0], *third_came]
    return place(source, here, parts)


def solution(mesh):
    placed = (P("atom", None, "fit", None), P("atom", None), P(None, "atom"), P())
    return jax.shard_map(
        per_device, mesh=mesh, in_specs=placed, out_specs=P(("atom", "fit"), None), check_vma=False
    )
```

time: 679 us -> 264 us (0.39)
  waiting for transfers between devices: 400 us -> 96.3 us
  local copies, waits for them, and re-layouts: 141 us -> 14.5 us
  Pallas kernels: 0 us -> 99.4 us
  matrix products: 51.9 us -> 0 us
  starting transfers between devices: 5.26 us -> 48.8 us
  other arithmetic: 35.7 us -> 2.58 us
  blocking collectives: 28.2 us -> 0 us
  between operations: 13.6 us -> 0.47 us
    all_to_all x1 -> x3, waiting for transfers between devices: 278 us -> 12.4 us  [the longest x1 12.4 us: per_device(): lax.all_to_all(jnp.broadcast_to(mine[None], (groups,) + mine.shape), 'ato...]
    reduce_scatter x1 -> x0, waiting for transfers between devices: 122 us -> none  [per_device(): lax.psum_scatter(partial_value, 'fit', scatter_dimension=0, tiled=True)]
    pallas_call x0 -> x13, Pallas kernels: none -> 99.4 us  [the longest x4 41.5 us: product(): pl.pallas_call(functools.partial(product_kernel, scale, jobs, len(sources...]
    ppermute x0 -> x19, waiting for transfers between devices: none -> 83.8 us  [the longest x14 72.2 us: send(): return lax.ppermute(payload, 'atom', route)]
    gather x4 -> x2, local copies, waits for them, and re-layouts: 63.7 us -> 1.21 us  [the longest x1 0.62 us: per_device(): picked = jnp.take(everyone, tensor_pattern.reshape(-1), axis=0)]
    dot_general x4 -> x0, matrix products: 51.9 us -> none  [the longest x1 20.9 us: per_device(): jnp.einsum('rf,scbf->rscb', own_rows, arrived, preferred_element_type=jnp...]
    reshape x2 -> x4, local copies, waits for them, and re-layouts: 50.9 us -> 1.02 us  [the longest x1 0.84 us: per_device(): picked.reshape(NBD, KB, 2 * NOCC, 32).transpose(0, 2, 1, 3)]
    all_gather x1 -> x0, blocking collectives: 28.2 us -> none  [per_device(): all_coeff = lax.all_gather(coefficients, 'atom', axis=1, tiled=True)]
  transfers between devices with their start and end apart: 2 -> 22, of which waited for: 2 -> 12; matrix products, arithmetic and copies ran while one was open for 3% -> 3% of each run, Pallas kernels for 0% -> 27%
where the time goes in v2:
time: 264 us; the launch traced here: 262 us
  Pallas kernels  99.4 us (38%)
  waiting for transfers between devices  96.3 us (36%)
  starting transfers between devices  48.8 us (18%)
  local copies, waits for them, and re-layouts  14.5 us (5%)
    ppermute x14, waiting for transfers between devices, send(): return lax.ppermute(payload, 'atom', route)  72.2 us
    pallas_call x4, Pallas kernels, product(): pl.pallas_call(functools.partial(product_kernel, scale, jobs, len(sources...  41.5 us
    pallas_call x3, Pallas kernels, pack(): pl.pallas_call(functools.partial(pack_kernel, jobs, len(operands)), in_sp...  18.2 us
    pallas_call x1, Pallas kernels, fit_rows(): pl.pallas_call(fit_kernel, grid=(NBD // 2,), in_specs=[pl.BlockSpec((2, K...  14.7 us
    ppermute x14, starting transfers between devices, send(): return lax.ppermute(payload, 'atom', route)  13.7 us
    all_to_all x1, waiting for transfers between devices, per_device(): lax.all_to_all(jnp.broadcast_to(mine[None], (groups,) + mine.shape), 'ato...  12.4 us
    pallas_call x2, Pallas kernels, sum_pieces(): pl.pallas_call(sum_kernel, grid=(count // TILES,), in_specs=[pl.BlockSpec...  9.83 us
    all_to_all x1, starting transfers between devices, per_device(): second_came = lax.all_to_all(partial, 'fit', 0, 0, tiled=True)  9.69 us
  transfers between devices with their start and end apart: 22, of which 12 were waited for; matrix products, arithmetic and copies ran while one was open for 3% of the time, Pallas kernels for 27%

profile of v2, /device:TPU:1, one launch (start us, length us, event | category | flops | bytes accessed | tf_op | source)
XLA Modules:
  0.0 262.0 jit_solution(4747003105199774756)
XLA Ops:
  3.3 8.6 %all-to-all-start = ((bf16[16,2,12288]{2,1,0:T(2,128)(2,1)}), bf16[16,2,12288]{2,1,0:T(2,128)(2,1)S(1)}, u32[]{:S(2)}, u32[]{:S(2)}) async-start(bf16[16,2,12288]{2,1,0:T(2,128)(2,1)} %reshape.119), calls=%async_computation | async-start | bytes 1572864 | tf_op jit(solution)/shard_map/all_to_all | solution.py:377
  12.2 12.4 %all-to-all-done = bf16[16,2,12288]{2,1,0:T(2,128)(2,1)S(1)} async-done(((bf16[16,2,12288]{2,1,0:T(2,128)(2,1)}), bf16[16,2,12288]{2,1,0:T(2,128)(2,1)S(1)}, u32[]{:S(2)}, u32[]{:S(2)}) %all-to-all-start) | async-done | bytes 786464 | tf_op jit(solution)/shard_map/all_to_all | solution.py:377
  27.3 14.7 %shard_map.64 = bf16[2,12,64,768]{3,2,1,0:T(8,128)(2,1)} custom-call(bf16[12,4,48,4096]{3,2,1,0:T(8,128)(2,1)} %tile_ref.1, bf16[12,64,128]{2,1,0:T(8,128)(2,1)} %copy.41.coeff_ref), custom_call_target="tpu_custom_call" | custom-call | tf_op jit(solution)/shard_map/pallas_call | solution.py:97
  49.5 6.9 %shard_map.65 = (bf16[4,18,96,128]{3,2,1,0:T(8,128)(2,1)}, bf16[4,18,96,128]{3,2,1,0:T(8,128)(2,1)}) custom-call(s32[16,6]{1,0:T(8,128)} %copy.44.index_ref, s32[2]{0:T(128)} %pad_add_fusion.here_ref, bf16[2,768,768]{2,1,0:T(8,128)(2,1)} %bitcast.33, bf16[24,64,768]{2,1,0:T(8,128)(2,1)} %bitcast.34), custom_call_target="tpu_custom_call" | custom-call | bytes 1048576 | tf_op jit(solution)/shard_map/pallas_call | solution.py:223
  56.4 36.6 %collective-permute-done.3.refs_3_ = bf16[24,64,768]{2,1,0:T(8,128)(2,1)S(1)} collective-permute-done((bf16[24,64,768]{2,1,0:T(8,128)(2,1)}, bf16[24,64,768]{2,1,0:T(8,128)(2,1)S(1)}, u32[]{:S(2)}, u32[]{:S(2)}) %collective-permute-start.3) | collective-permute-done | bytes 2359328 | tf_op jit(solution)/shard_map/ppermute | solution.py:401
  96.2 8.7 %shard_map.66 = (bf16[24,64,768]{2,1,0:T(8,128)(2,1)}, bf16[24,64,768]{2,1,0:T(8,128)(2,1)}, bf16[24,64,768]{2,1,0:T(8,128)(2,1)}, bf16[24,64,768]{2,1,0:T(8,128)(2,1)}) custom-call(s32[16,6]{1,0:T(8,128)} %copy.44.index_ref, bf16[24,64,768]{2,1,0:T(8,128)(2,1)} %collective-permute-done.refs_0_, bf16[24,64,768]{2,1,0:T(8,128)(2,1)} %collective-permute-done.1.refs_1_, ...), custom_call_target="tpu_custom_call" | custom-call | bytes 1048576 | tf_op jit(solution)/shard_map/pallas_call | solution.py:135
  110.0 10.1 %shard_map.67 = (bf16[4,18,96,128]{3,2,1,0:T(8,128)(2,1)}, bf16[4,18,96,128]{3,2,1,0:T(8,128)(2,1)}) custom-call(s32[16,6]{1,0:T(8,128)} %copy.44.index_ref, s32[2]{0:T(128)} %pad_add_fusion.here_ref, bf16[2,768,768]{2,1,0:T(8,128)(2,1)} %bitcast.35, ...), custom_call_target="tpu_custom_call", output_to_operand_aliasing={{0}: (8, {}), {1}: (9, {})} | custom-call | bytes 1048576 | tf_op jit(solution)/shard_map/pallas_call | solution.py:223
  120.2 4.1 %collective-permute-start.4 = (bf16[4,18,96,128]{3,2,1,0:T(8,128)(2,1)}, bf16[4,18,96,128]{3,2,1,0:T(8,128)(2,1)S(1)}, u32[]{:S(2)}, u32[]{:S(2)}) collective-permute-start(bf16[4,18,96,128]{3,2,1,0:T(8,128)(2,1)} %get-tuple-element.28), channel_id=1, source_target_pairs={{0,1},{1,0},{2,3},{3,2},{4,5},{5,4},{6,7},{7,6},{8,9},{9,8},{10,11... | collective-permute-start | bytes 5308424 | tf_op jit(solution)/shard_map/ppermute | solution.py:418
  124.2 3.5 %collective-permute-done.4.came_ref = bf16[4,18,96,128]{3,2,1,0:T(8,128)(2,1)S(1)} collective-permute-done((bf16[4,18,96,128]{3,2,1,0:T(8,128)(2,1)}, bf16[4,18,96,128]{3,2,1,0:T(8,128)(2,1)S(1)}, u32[]{:S(2)}, u32[]{:S(2)}) %collective-permute-start.4) | collective-permute-done | bytes 1769504 | tf_op jit(solution)/shard_map/ppermute | solution.py:418
  129.0 5.1 %shard_map.68.refs_4_ = bf16[4,18,96,128]{3,2,1,0:T(8,128)(2,1)} custom-call(bf16[4,18,96,128]{3,2,1,0:T(8,128)(2,1)} %get-tuple-element.27.keep_ref, bf16[4,18,96,128]{3,2,1,0:T(8,128)(2,1)} %copy-done.2), custom_call_target="tpu_custom_call" | custom-call | bytes 1048576 | tf_op jit(solution)/shard_map/pallas_call | solution.py:257
  134.1 4.4 %all-to-all-start.1 = ((bf16[4,18,96,128]{3,2,1,0:T(8,128)(2,1)}), bf16[4,18,96,128]{3,2,1,0:T(8,128)(2,1)}, u32[]{:S(2)}, u32[]{:S(2)}) async-start(bf16[4,18,96,128]{3,2,1,0:T(8,128)(2,1)} %shard_map.68.refs_4_), calls=%async_computation.1 | async-start | bytes 3538944 | tf_op jit(solution)/shard_map/all_to_all | solution.py:429
  138.5 16.5 %collective-permute-done.6.refs_1_ = bf16[24,64,768]{2,1,0:T(8,128)(2,1)} collective-permute-done((bf16[24,64,768]{2,1,0:T(8,128)(2,1)}, bf16[24,64,768]{2,1,0:T(8,128)(2,1)}, u32[]{:S(2)}, u32[]{:S(2)}) %collective-permute-start.6) | collective-permute-done | bytes 2359328 | tf_op jit(solution)/shard_map/ppermute | solution.py:401
  155.0 3.1 %collective-permute-done.7.refs_2_ = bf16[24,64,768]{2,1,0:T(8,128)(2,1)} collective-permute-done((bf16[24,64,768]{2,1,0:T(8,128)(2,1)}, bf16[24,64,768]{2,1,0:T(8,128)(2,1)}, u32[]{:S(2)}, u32[]{:S(2)}) %collective-permute-start.7) | collective-permute-done | bytes 2359328 | tf_op jit(solution)/shard_map/ppermute | solution.py:401
  160.2 6.6 %shard_map.70 = (bf16[12,64,768]{2,1,0:T(8,128)(2,1)}, bf16[12,64,768]{2,1,0:T(8,128)(2,1)}, bf16[12,64,768]{2,1,0:T(8,128)(2,1)}, bf16[12,64,768]{2,1,0:T(8,128)(2,1)}, bf16[6,64,768]{2,1,0:T(8,128)(2,1)}) custom-call(s32[16,6]{1,0:T(8,128)} %copy.44.index_ref, bf16[24,64,768]{2,1,0:T(8,128)(2,1)} %collective-permute-done.5.refs_0_, ...), custom_call_target="tpu_custom_call" | custom-call | bytes 1048576 | tf_op jit(solution)/shard_map/pallas_call | solution.py:135
  172.4 12.8 %shard_map.71.refs_1_ = bf16[8,18,96,128]{3,2,1,0:T(8,128)(2,1)} custom-call(s32[16,6]{1,0:T(8,128)} %copy.44.index_ref, s32[2]{0:T(128)} %pad_add_fusion.here_ref, bf16[2,768,768]{2,1,0:T(8,128)(2,1)} %bitcast.36, bf16[24,64,768]{2,1,0:T(8,128)(2,1)} %collective-permute-done.5.refs_0_, bf16[24,64,768]{2,1,0:T(8,128)(2,1)} %collective-permute-done.6.refs_1_, ...), custom_call_target="tpu_custom_call" | custom-call | bytes 1048576 | tf_op jit(solution)/shard_map/pallas_call | solution.py:223
  188.1 9.7 %all-to-all-start.2 = ((bf16[8,18,96,128]{3,2,1,0:T(8,128)(2,1)}), bf16[8,18,96,128]{3,2,1,0:T(8,128)(2,1)}, u32[]{:S(2)}, u32[]{:S(2)}) async-start(bf16[8,18,96,128]{3,2,1,0:T(8,128)(2,1)} %shard_map.71.refs_1_), calls=%async_computation.2 | async-start | bytes 7077888 | tf_op jit(solution)/shard_map/all_to_all | solution.py:464
  197.8 8.0 %collective-permute-done.14.refs_5_ = bf16[6,64,768]{2,1,0:T(8,128)(2,1)} collective-permute-done((bf16[6,64,768]{2,1,0:T(8,128)(2,1)}, bf16[6,64,768]{2,1,0:T(8,128)(2,1)}, u32[]{:S(2)}, u32[]{:S(2)}) %collective-permute-start.14) | collective-permute-done | bytes 589856 | tf_op jit(solution)/shard_map/ppermute | solution.py:401
  209.2 11.6 %shard_map.74 = (bf16[4,15,96,128]{3,2,1,0:T(8,128)(2,1)}, bf16[4,15,96,128]{3,2,1,0:T(8,128)(2,1)}) custom-call(s32[16,6]{1,0:T(8,128)} %copy.44.index_ref, s32[2]{0:T(128)} %pad_add_fusion.here_ref, bf16[2,768,768]{2,1,0:T(8,128)(2,1)} %bitcast.37, bf16[12,64,768]{2,1,0:T(8,128)(2,1)} %collective-permute-done.9.refs_0_, bf16[12,64,768]{2,1,0:T(8,128)(2,1)} %copy-done.12, ...), custom_call_target="tpu_custom_call" | custom-call | flops 999999995904 | bytes 1048576 | tf_op jit(solution)/shard_map/pallas_call | solution.py:223
  220.9 3.6 %collective-permute-start.15 = (bf16[4,15,96,128]{3,2,1,0:T(8,128)(2,1)}, bf16[4,15,96,128]{3,2,1,0:T(8,128)(2,1)S(1)}, u32[]{:S(2)}, u32[]{:S(2)}) collective-permute-start(bf16[4,15,96,128]{3,2,1,0:T(8,128)(2,1)} %get-tuple-element.38), channel_id=1, source_target_pairs={{0,1},{1,0},{2,3},{3,2},{4,5},{5,4},{6,7},{7,6},{8,9},{9,8},{10,11... | collective-permute-start | bytes 4423688 | tf_op jit(solution)/shard_map/ppermute | solution.py:418
  228.7 4.5 %shard_map.75 = (f32[15,96,128]{2,1,0:T(8,128)}, bf16[15,96,128]{2,1,0:T(8,128)(2,1)}, bf16[15,96,128]{2,1,0:T(8,128)(2,1)}, bf16[15,96,128]{2,1,0:T(8,128)(2,1)}) custom-call(s32[2]{0:T(128)} %pad_add_fusion.here_ref, bf16[4,15,96,128]{3,2,1,0:T(8,128)(2,1)} %get-tuple-element.37.keep_ref, bf16[4,15,96,128]{3,2,1,0:T(8,128)(2,1)} %copy-done.3), custom_call_target="tpu_custom_call" | custom-call | bytes 1048576 | tf_op jit(solution)/shard_map/pallas_call | solution.py:273
  239.6 4.7 %shard_map.69.refs_0_ = bf16[2,18,96,128]{3,2,1,0:T(8,128)(2,1)} custom-call(bf16[4,18,96,128]{3,2,1,0:T(8,128)(2,1)} %all-to-all-done.1.given_ref.refs_6_), custom_call_target="tpu_custom_call" | custom-call | bytes 1048576 | tf_op jit(solution)/shard_map/pallas_call | solution.py:296
  244.3 5.2 %shard_map.72.refs_1_ = bf16[2,18,96,128]{3,2,1,0:T(8,128)(2,1)} custom-call(bf16[8,18,96,128]{3,2,1,0:T(8,128)(2,1)} %all-to-all-done.2.given_ref), custom_call_target="tpu_custom_call" | custom-call | bytes 1048576 | tf_op jit(solution)/shard_map/pallas_call | solution.py:296
  249.5 6.0 %collective-permute-done.17.refs_4_ = bf16[15,96,128]{2,1,0:T(8,128)(2,1)S(1)} collective-permute-done((bf16[15,96,128]{2,1,0:T(8,128)(2,1)}, bf16[15,96,128]{2,1,0:T(8,128)(2,1)S(1)}, u32[]{:S(2)}, u32[]{:S(2)}) %collective-permute-start.17) | collective-permute-done | bytes 368672 | tf_op jit(solution)/shard_map/ppermute | solution.py:424
  256.3 5.6 %shard_map.76 = bf16[96,12288]{1,0:T(8,128)(2,1)} custom-call(s32[96]{0:T(128)} %slice.12.left_ref, s32[96]{0:T(128)} %slice.13.right_ref, s32[2]{0:T(128)} %pad_add_fusion.here_ref, bf16[2,18,96,128]{3,2,1,0:T(8,128)(2,1)} %shard_map.69.refs_0_, bf16[2,18,96,128]{3,2,1,0:T(8,128)(2,1)} %shard_map.72.refs_1_, f32[15,96,128]{2,1,0:T(8,128)} %get-tuple-element.39.refs_2_, ...), custom_call_target="tpu_custom_call" | custom-call | tf_op jit(solution)/shard_map/pallas_call | solution.py:357
  (104 shorter events, 48.4 us)
Async XLA Ops:
  3.3 21.4 %all-to-all-start = ((bf16[16,2,12288]{2,1,0:T(2,128)(2,1)}), bf16[16,2,12288]{2,1,0:T(2,128)(2,1)S(1)}, u32[]{:S(2)}, u32[]{:S(2)}) async-start(bf16[16,2,12288]{2,1,0:T(2,128)(2,1)} %reshape.119), calls=%async_computation | async-start | bytes 1572864 | tf_op jit(solution)/shard_map/all_to_all | solution.py:377
  27.3 17.7 %copy-start.8 = (s32[192,4]{0,1:T(4,128)S(1)}, s32[192,4]{0,1:T(4,128)}, u32[]{:S(2)}) copy-start(s32[192,4]{0,1:T(4,128)} %param.9) | copy-start | bytes 9220
  42.0 51.0 %collective-permute-start.3 = (bf16[24,64,768]{2,1,0:T(8,128)(2,1)}, bf16[24,64,768]{2,1,0:T(8,128)(2,1)S(1)}, u32[]{:S(2)}, u32[]{:S(2)}) collective-permute-start(bf16[24,64,768]{2,1,0:T(8,128)(2,1)} %bitcast.29), channel_id=1, source_target_pairs={{0,24},{8,0},{16,8},{24,16},{32,56},{40,32},{48,40},{56,48},{64,88... | collective-permute-start | bytes 7077896 | tf_op jit(solution)/shard_map/ppermute | solution.py:401
  43.6 52.6 %collective-permute-start.2 = (bf16[24,64,768]{2,1,0:T(8,128)(2,1)}, bf16[24,64,768]{2,1,0:T(8,128)(2,1)}, u32[]{:S(2)}, u32[]{:S(2)}) collective-permute-start(bf16[24,64,768]{2,1,0:T(8,128)(2,1)} %bitcast.30), channel_id=1, source_target_pairs={{0,8},{8,16},{16,24},{24,0},{32,40},{40,48},{48,56},{56,32},{64,72... | collective-permute-start | bytes 7077896 | tf_op jit(solution)/shard_map/ppermute | solution.py:401
  43.6 52.6 %collective-permute-start.1 = (bf16[24,64,768]{2,1,0:T(8,128)(2,1)}, bf16[24,64,768]{2,1,0:T(8,128)(2,1)}, u32[]{:S(2)}, u32[]{:S(2)}) collective-permute-start(bf16[24,64,768]{2,1,0:T(8,128)(2,1)} %bitcast.31), channel_id=1, source_target_pairs={{0,96},{8,104},{16,112},{24,120},{32,0},{40,8},{48,16},{56,24},{64... | collective-permute-start | bytes 7077896 | tf_op jit(solution)/shard_map/ppermute | solution.py:401
  44.8 51.4 %collective-permute-start = (bf16[24,64,768]{2,1,0:T(8,128)(2,1)}, bf16[24,64,768]{2,1,0:T(8,128)(2,1)}, u32[]{:S(2)}, u32[]{:S(2)}) collective-permute-start(bf16[24,64,768]{2,1,0:T(8,128)(2,1)} %bitcast.32), channel_id=1, source_target_pairs={{0,32},{8,40},{16,48},{24,56},{32,64},{40,72},{48,80},{56,88},{64,... | collective-permute-start | bytes 7077896 | tf_op jit(solution)/shard_map/ppermute | solution.py:401
  104.9 50.0 %collective-permute-start.6 = (bf16[24,64,768]{2,1,0:T(8,128)(2,1)}, bf16[24,64,768]{2,1,0:T(8,128)(2,1)}, u32[]{:S(2)}, u32[]{:S(2)}) collective-permute-start(bf16[24,64,768]{2,1,0:T(8,128)(2,1)} %get-tuple-element.29), channel_id=1, source_target_pairs={{0,96},{8,104},{16,112},{24,120},{32,0},{40,8},{48,16},{56,24},{64... | collective-permute-start | bytes 7077896 | tf_op jit(solution)/shard_map/ppermute | solution.py:401
  106.4 51.7 %collective-permute-start.7 = (bf16[24,64,768]{2,1,0:T(8,128)(2,1)}, bf16[24,64,768]{2,1,0:T(8,128)(2,1)}, u32[]{:S(2)}, u32[]{:S(2)}) collective-permute-start(bf16[24,64,768]{2,1,0:T(8,128)(2,1)} %get-tuple-element.30), channel_id=1, source_target_pairs={{0,8},{8,16},{16,24},{24,0},{32,40},{40,48},{48,56},{56,32},{64,72... | collective-permute-start | bytes 7077896 | tf_op jit(solution)/shard_map/ppermute | solution.py:401
  106.4 51.7 %collective-permute-start.8 = (bf16[24,64,768]{2,1,0:T(8,128)(2,1)}, bf16[24,64,768]{2,1,0:T(8,128)(2,1)S(1)}, u32[]{:S(2)}, u32[]{:S(2)}) collective-permute-start(bf16[24,64,768]{2,1,0:T(8,128)(2,1)} %get-tuple-element.31), channel_id=1, source_target_pairs={{0,24},{8,0},{16,8},{24,16},{32,56},{40,32},{48,40},{56,48},{64,88... | collective-permute-start | bytes 7077896 | tf_op jit(solution)/shard_map/ppermute | solution.py:401
  109.1 51.1 %collective-permute-start.5 = (bf16[24,64,768]{2,1,0:T(8,128)(2,1)}, bf16[24,64,768]{2,1,0:T(8,128)(2,1)}, u32[]{:S(2)}, u32[]{:S(2)}) collective-permute-start(bf16[24,64,768]{2,1,0:T(8,128)(2,1)} %get-tuple-element.25.refs_4_), channel_id=1, source_target_pairs={{0,32},{8,40},{16,48},{24,56},{32,64},{40,72},{48,80},{56,88},{64,... | collective-permute-start | bytes 7077896 | tf_op jit(solution)/shard_map/ppermute | solution.py:401
  120.2 7.6 %collective-permute-start.4 = (bf16[4,18,96,128]{3,2,1,0:T(8,128)(2,1)}, bf16[4,18,96,128]{3,2,1,0:T(8,128)(2,1)S(1)}, u32[]{:S(2)}, u32[]{:S(2)}) collective-permute-start(bf16[4,18,96,128]{3,2,1,0:T(8,128)(2,1)} %get-tuple-element.28), channel_id=1, source_target_pairs={{0,1},{1,0},{2,3},{3,2},{4,5},{5,4},{6,7},{7,6},{8,9},{9,8},{10,11... | collective-permute-start | bytes 5308424 | tf_op jit(solution)/shard_map/ppermute | solution.py:418
  134.1 54.0 %all-to-all-start.1 = ((bf16[4,18,96,128]{3,2,1,0:T(8,128)(2,1)}), bf16[4,18,96,128]{3,2,1,0:T(8,128)(2,1)}, u32[]{:S(2)}, u32[]{:S(2)}) async-start(bf16[4,18,96,128]{3,2,1,0:T(8,128)(2,1)} %shard_map.68.refs_4_), calls=%async_computation.1 | async-start | bytes 3538944 | tf_op jit(solution)/shard_map/all_to_all | solution.py:429
  166.8 21.1 %collective-permute-start.13 = (bf16[6,64,768]{2,1,0:T(8,128)(2,1)}, bf16[6,64,768]{2,1,0:T(8,128)(2,1)}, u32[]{:S(2)}, u32[]{:S(2)}) collective-permute-start(bf16[6,64,768]{2,1,0:T(8,128)(2,1)} %get-tuple-element.36), channel_id=1, source_target_pairs={{0,16},{8,24},{16,0},{24,8},{32,48},{40,56},{48,32},{56,40},{64,80... | collective-permute-start | bytes 1769480 | tf_op jit(solution)/shard_map/ppermute | solution.py:401
  168.2 39.2 %collective-permute-start.10 = (bf16[12,64,768]{2,1,0:T(8,128)(2,1)}, bf16[12,64,768]{2,1,0:T(8,128)(2,1)S(1)}, u32[]{:S(2)}, u32[]{:S(2)}) collective-permute-start(bf16[12,64,768]{2,1,0:T(8,128)(2,1)} %get-tuple-element.33), channel_id=1, source_target_pairs={{0,24},{8,0},{16,8},{24,16},{32,56},{40,32},{48,40},{56,48},{64,88... | collective-permute-start | bytes 3538952 | tf_op jit(solution)/shard_map/ppermute | solution.py:401
  168.9 38.6 %collective-permute-start.11 = (bf16[12,64,768]{2,1,0:T(8,128)(2,1)}, bf16[12,64,768]{2,1,0:T(8,128)(2,1)S(1)}, u32[]{:S(2)}, u32[]{:S(2)}) collective-permute-start(bf16[12,64,768]{2,1,0:T(8,128)(2,1)} %get-tuple-element.34), channel_id=1, source_target_pairs={{0,32},{8,40},{16,48},{24,56},{32,64},{40,72},{48,80},{56,88},{64,... | collective-permute-start | bytes 3538952 | tf_op jit(solution)/shard_map/ppermute | solution.py:401
  169.9 37.6 %collective-permute-start.12 = (bf16[12,64,768]{2,1,0:T(8,128)(2,1)}, bf16[12,64,768]{2,1,0:T(8,128)(2,1)S(1)}, u32[]{:S(2)}, u32[]{:S(2)}) collective-permute-start(bf16[12,64,768]{2,1,0:T(8,128)(2,1)} %get-tuple-element.35), channel_id=1, source_target_pairs={{0,96},{8,104},{16,112},{24,120},{32,0},{40,8},{48,16},{56,24},{64... | collective-permute-start | bytes 3538952 | tf_op jit(solution)/shard_map/ppermute | solution.py:401
  171.5 37.0 %collective-permute-start.9 = (bf16[12,64,768]{2,1,0:T(8,128)(2,1)}, bf16[12,64,768]{2,1,0:T(8,128)(2,1)}, u32[]{:S(2)}, u32[]{:S(2)}) collective-permute-start(bf16[12,64,768]{2,1,0:T(8,128)(2,1)} %get-tuple-element.32.refs_4_), channel_id=1, source_target_pairs={{0,8},{8,16},{16,24},{24,0},{32,40},{40,48},{48,56},{56,32},{64,72... | collective-permute-start | bytes 3538952 | tf_op jit(solution)/shard_map/ppermute | solution.py:401
  188.0 17.8 %collective-permute-start.14 = (bf16[6,64,768]{2,1,0:T(8,128)(2,1)}, bf16[6,64,768]{2,1,0:T(8,128)(2,1)}, u32[]{:S(2)}, u32[]{:S(2)}) collective-permute-start(bf16[6,64,768]{2,1,0:T(8,128)(2,1)} %shard_map.73), channel_id=1, source_target_pairs={{0,64},{8,72},{16,80},{24,88},{32,96},{40,104},{48,112},{56,120},{... | collective-permute-start | bytes 1769480 | tf_op jit(solution)/shard_map/ppermute | solution.py:401
  188.1 56.2 %all-to-all-start.2 = ((bf16[8,18,96,128]{3,2,1,0:T(8,128)(2,1)}), bf16[8,18,96,128]{3,2,1,0:T(8,128)(2,1)}, u32[]{:S(2)}, u32[]{:S(2)}) async-start(bf16[8,18,96,128]{3,2,1,0:T(8,128)(2,1)} %shard_map.71.refs_1_), calls=%async_computation.2 | async-start | bytes 7077888 | tf_op jit(solution)/shard_map/all_to_all | solution.py:464
  220.9 17.3 %copy-start.11 = (pred[192]{0:T(512)(128)(4,1)S(1)}, pred[192]{0:T(512)(128)(4,1)}, u32[]{:S(2)}) copy-start(pred[192]{0:T(512)(128)(4,1)} %copy-done.10) | copy-start | bytes 580
  220.9 6.7 %collective-permute-start.15 = (bf16[4,15,96,128]{3,2,1,0:T(8,128)(2,1)}, bf16[4,15,96,128]{3,2,1,0:T(8,128)(2,1)S(1)}, u32[]{:S(2)}, u32[]{:S(2)}) collective-permute-start(bf16[4,15,96,128]{3,2,1,0:T(8,128)(2,1)} %get-tuple-element.38), channel_id=1, source_target_pairs={{0,1},{1,0},{2,3},{3,2},{4,5},{5,4},{6,7},{7,6},{8,9},{9,8},{10,11... | collective-permute-start | bytes 4423688 | tf_op jit(solution)/shard_map/ppermute | solution.py:418
  233.2 16.3 %collective-permute-start.16 = (bf16[15,96,128]{2,1,0:T(8,128)(2,1)}, bf16[15,96,128]{2,1,0:T(8,128)(2,1)S(1)}, u32[]{:S(2)}, u32[]{:S(2)}) collective-permute-start(bf16[15,96,128]{2,1,0:T(8,128)(2,1)} %get-tuple-element.40), channel_id=1, source_target_pairs={{0,2},{1,3},{2,4},{3,5},{4,6},{5,7},{6,0},{7,1},{8,10},{9,11},{10,... | collective-permute-start | bytes 1105928 | tf_op jit(solution)/shard_map/ppermute | solution.py:424
  234.4 21.1 %collective-permute-start.17 = (bf16[15,96,128]{2,1,0:T(8,128)(2,1)}, bf16[15,96,128]{2,1,0:T(8,128)(2,1)S(1)}, u32[]{:S(2)}, u32[]{:S(2)}) collective-permute-start(bf16[15,96,128]{2,1,0:T(8,128)(2,1)} %get-tuple-element.41), channel_id=1, source_target_pairs={{0,4},{1,5},{2,6},{3,7},{4,0},{5,1},{6,2},{7,3},{8,12},{9,13},{10,... | collective-permute-start | bytes 1105928 | tf_op jit(solution)/shard_map/ppermute | solution.py:424
  236.9 18.6 %collective-permute-start.18 = (bf16[15,96,128]{2,1,0:T(8,128)(2,1)}, bf16[15,96,128]{2,1,0:T(8,128)(2,1)S(1)}, u32[]{:S(2)}, u32[]{:S(2)}) collective-permute-start(bf16[15,96,128]{2,1,0:T(8,128)(2,1)} %get-tuple-element.42), channel_id=1, source_target_pairs={{0,6},{1,7},{2,0},{3,1},{4,2},{5,3},{6,4},{7,5},{8,14},{9,15},{10,... | collective-permute-start | bytes 1105928 | tf_op jit(solution)/shard_map/ppermute | solution.py:424
  (13 other events, 47.5 us)

commit v3 on v2

--- a/solution.py
+++ b/solution.py
@@ -72,7 +72,30 @@
 BASE_OF = np.array([[BASE[minus(me, h)] for h in PLACES] for me in PLACES], dtype=np.int32)
 
 
-def fit_kernel(tile_ref, coeff_ref, out_ref, lines):
+def spread_matrices():
+    table = np.zeros((KB, 128, 256), np.float32)
+    for k in range(KB):
+        for l in range(BS):
+            table[k, l, (l % 2) * 128 + k * 32 + l // 2] = 1.0
+    return table
+
+
+def fit_kernel(where_ref, tile_ref, coeff_ref, spread_ref, out_ref, lines, chosen):
+    step = pl.program_id(0)
+
+    @pl.when(step == 0)
+    def _():
+        for n in range(NBD):
+            total = jnp.zeros((NOCC, 256), jnp.float32)
+            for k in range(KB):
+                lane = pl.ds(pl.multiple_of(where_ref[1, n * KB + k] * 128, 128), 128)
+                tile = coeff_ref[where_ref[0, n * KB + k], :, lane].astype(jnp.float32)
+                odd = where_ref[2, n * KB + k] == 1
+                tile = jnp.where(odd, pltpu.roll(tile, BS, 1), tile).astype(jnp.bfloat16)
+                total += jnp.dot(tile, spread_ref[k], preferred_element_type=jnp.float32)
+            both = jnp.concatenate([total[:, 0:128], total[:, 128:256]], axis=0)
+            chosen[n] = both.astype(jnp.bfloat16)
+
     for m in range(2):
         for k in range(KB):
             for pair in range(BS // 2):
@@ -84,7 +107,7 @@
             parts = []
             for p in range(group * 4, group * 4 + 4):
                 rows = lines[m, pl.ds(p, 128, stride=GAP), :].astype(jnp.bfloat16)
-                product = jnp.dot(coeff_ref[m], rows, preferred_element_type=jnp.float32)
+                product = jnp.dot(chosen[2 * step + m], rows, preferred_element_type=jnp.float32)
                 parts.append(product[0:NOCC] + pltpu.roll(product[NOCC:], 64, 1))
             both.append(jnp.concatenate(parts, axis=0)[:, 0:BS])
         turned = jnp.concatenate(both, axis=1).T.astype(jnp.bfloat16)
@@ -93,19 +116,26 @@
         out_ref[group // 6, 1, :, place : place + 128] = turned[BS:]
 
 
-def fit_rows(three_centre, picked):
+def fit_rows(three_centre, where, everyone):
+    spread = jnp.asarray(spread_matrices(), jnp.bfloat16)
     return pl.pallas_call(
         fit_kernel,
         grid=(NBD // 2,),
         in_specs=[
+            pl.BlockSpec(memory_space=pltpu.SMEM),
             pl.BlockSpec((2, KB, NP, BS * BS), lambda g: (g, 0, 0, 0)),
-            pl.BlockSpec((2, 2 * NOCC, 128), lambda g: (g, 0, 0)),
+            pl.BlockSpec(everyone.shape, lambda g: (0, 0, 0)),
+            pl.BlockSpec(spread.shape, lambda g: (0, 0, 0)),
         ],
         out_specs=pl.BlockSpec((2, 2, BS, HALF), lambda g: (0, g, 0, 0)),
         out_shape=jax.ShapeDtypeStruct((2, NBD, BS, HALF), jnp.bfloat16),
-        scratch_shapes=[pltpu.VMEM((2, KB * 32 * GAP, 128), jnp.float32)],
-        compiler_params=pltpu.CompilerParams(vmem_limit_bytes=58 * MIB),
-    )(three_centre, picked)
+        scratch_shapes=[
+            pltpu.VMEM((2, KB * 32 * GAP, 128), jnp.float32),
+            pltpu.VMEM((NBD, 2 * NOCC, 128), jnp.bfloat16),
+        ],
+        compiler_params=pltpu.CompilerParams(vmem_limit_bytes=58 * MIB),
+        cost_estimate=pl.CostEstimate(flops=2**30, bytes_accessed=20 * MIB, transcendentals=0),
+    )(where, three_centre, everyone, spread)
 
 
 def pack_kernel(jobs, n_in, index_ref, *refs):
@@ -241,7 +271,7 @@
 def add_kernel(here_ref, keep_ref, came_ref, own_ref, *send_refs):
     x = here_ref[1] >> 1
     own_ref[...] = keep_ref[x].astype(jnp.float32) + came_ref[x].astype(jnp.float32)
-    for shift, send_ref in zip((1, 2, 3), send_refs, strict=True):
+    for shift, send_ref in zip((2, 1, 3), send_refs, strict=True):
         there = (x + shift) & (SIDE - 1)
         value = keep_ref[there].astype(jnp.float32) + came_ref[there].astype(jnp.float32)
         send_ref[...] = value.astype(jnp.bfloat16)
@@ -267,12 +297,13 @@
 
 def add_cores(here, keep, came):
     count = keep.shape[1]
-    block = pl.BlockSpec((FIT // 2, TILES, PIECE, 128), lambda j: (0, j, 0, 0))
-    out = pl.BlockSpec((TILES, PIECE, 128), lambda j: (j, 0, 0))
+    step = 5 if count % 5 == 0 else TILES
+    block = pl.BlockSpec((FIT // 2, step, PIECE, 128), lambda j: (0, j, 0, 0))
+    out = pl.BlockSpec((step, PIECE, 128), lambda j: (j, 0, 0))
     shape = (count, PIECE, 128)
     return pl.pallas_call(
         add_kernel,
-        grid=(count // TILES,),
+        grid=(count // step,),
         in_specs=[pl.BlockSpec(memory_space=pltpu.SMEM), block, block],
         out_specs=[out] * 4,
         out_shape=[jax.ShapeDtypeStruct(shape, jnp.float32)]
@@ -373,13 +404,11 @@
     groups = SIDE * SIDE
     me = lax.axis_index("atom")
     lane = lax.axis_index("fit")
-    mine = coefficients.reshape(NOCC, NBD, 32, 2).transpose(1, 3, 0, 2).reshape(NBD, 2 * NOCC, 32)
-    everyone = lax.all_to_all(
-        jnp.broadcast_to(mine[None], (groups,) + mine.shape), "atom", 0, 0, tiled=True
-    ).reshape(groups * NBD, 2 * NOCC, 32)
-    picked = jnp.take(everyone, tensor_pattern.reshape(-1), axis=0)
-    picked = picked.reshape(NBD, KB, 2 * NOCC, 32).transpose(0, 2, 1, 3).reshape(NBD, 2 * NOCC, 128)
-    own = fit_rows(three_centre, picked)
+    everyone = jnp.broadcast_to(coefficients[None], (groups,) + coefficients.shape)
+    everyone = lax.all_to_all(everyone, "atom", 0, 0, tiled=True)
+    partner = tensor_pattern.reshape(-1)
+    where = jnp.stack([partner // NBD, (partner % NBD) // 2, partner % 2]).astype(jnp.int32)
+    own = fit_rows(three_centre, where, everyone)
 
     by_group = readers.reshape(groups, NBD, 4)
     pairs = jnp.asarray(PAIRS)[me]
@@ -419,7 +448,7 @@
 
     def over_chips(pieces):
         sent = []
-        for shift, piece in zip((1, 2, 3), pieces, strict=True):
+        for shift, piece in zip((2, 1, 3), pieces, strict=True):
             route = [(n, (n + 2 * shift) % FIT) for n in range(FIT)]
             sent.append(lax.ppermute(piece, "fit", route))
         return sent

time: 264 us -> 262 us (level)
  local copies, waits for them, and re-layouts: 14.5 us -> 11.2 us
    unnamed x35 -> x33, local copies, waits for them, and re-layouts: 8.57 us -> 5.18 us
where the time goes in v3:
time: 262 us; the launch traced here: 261 us
  Pallas kernels  100 us (38%)
  waiting for transfers between devices  96.3 us (37%)
  starting transfers between devices  49.5 us (19%)
  local copies, waits for them, and re-layouts  11.2 us (4%)
  other arithmetic  3.09 us (1%)
    ppermute x14, waiting for transfers between devices, send(): return lax.ppermute(payload, 'atom', route)  71.7 us
    pallas_call x4, Pallas kernels, product(): pl.pallas_call(functools.partial(product_kernel, scale, jobs, len(sources...  41.9 us
    pallas_call x3, Pallas kernels, pack(): pl.pallas_call(functools.partial(pack_kernel, jobs, len(operands)), in_sp...  18.4 us
    pallas_call x1, Pallas kernels, fit_rows(): pl.pallas_call(fit_kernel, grid=(NBD // 2,), in_specs=[pl.BlockSpec(memor...  15.7 us
    ppermute x14, starting transfers between devices, send(): return lax.ppermute(payload, 'atom', route)  13.6 us
    all_to_all x1, waiting for transfers between devices, per_device(): everyone = lax.all_to_all(everyone, 'atom', 0, 0, tiled=True)  12 us
    all_to_all x1, starting transfers between devices, per_device(): second_came = lax.all_to_all(partial, 'fit', 0, 0, tiled=True)  9.94 us
    pallas_call x2, Pallas kernels, sum_pieces(): pl.pallas_call(sum_kernel, grid=(count // TILES,), in_specs=[pl.BlockSpec...  9.82 us
  transfers between devices with their start and end apart: 22, of which 12 were waited for; matrix products, arithmetic and copies ran while one was open for 3% of the time, Pallas kernels for 27%

profile of v3, /device:TPU:1, one launch (start us, length us, event | category | flops | bytes accessed | tf_op | source)
XLA Modules:
  0.0 260.8 jit_solution(18072104951995065657)
XLA Ops:
  1.8 8.6 %all-to-all-start = ((bf16[16,32,768]{2,1,0:T(8,128)(2,1)}), bf16[16,32,768]{2,1,0:T(8,128)(2,1)S(1)}, u32[]{:S(2)}, u32[]{:S(2)}) async-start(bf16[16,32,768]{2,1,0:T(8,128)(2,1)} %broadcast_in_dim.54), calls=%async_computation | async-start | bytes 1572864 | tf_op jit(solution)/shard_map/all_to_all | solution.py:408
  11.2 12.0 %all-to-all-done.coeff_ref = bf16[16,32,768]{2,1,0:T(8,128)(2,1)S(1)} async-done(((bf16[16,32,768]{2,1,0:T(8,128)(2,1)}), bf16[16,32,768]{2,1,0:T(8,128)(2,1)S(1)}, u32[]{:S(2)}, u32[]{:S(2)}) %all-to-all-start) | async-done | bytes 786464 | tf_op jit(solution)/shard_map/all_to_all | solution.py:408
  24.0 15.7 %shard_map.73 = bf16[2,12,64,768]{3,2,1,0:T(8,128)(2,1)} custom-call(s32[3,48]{1,0:T(4,128)} %pad_add_fusion.where_ref, bf16[12,4,48,4096]{3,2,1,0:T(8,128)(2,1)} %tile_ref.1, bf16[16,32,768]{2,1,0:T(8,128)(2,1)} %copy-done.2, bf16[4,128,256]{2,1,0:T(8,128)(2,1)} %constant.70.clone.spread_ref), custom_call_target="tpu_custom_call" | custom-call | flops 1073741824 | bytes 20971520 | tf_op jit(solution)/shard_map/pallas_call | solution.py:121
  47.2 6.9 %shard_map.74 = (bf16[4,18,96,128]{3,2,1,0:T(8,128)(2,1)}, bf16[4,18,96,128]{3,2,1,0:T(8,128)(2,1)}) custom-call(s32[16,6]{1,0:T(8,128)} %copy.29.index_ref, s32[2]{0:T(128)} %pad_add_fusion.1.here_ref, bf16[2,768,768]{2,1,0:T(8,128)(2,1)} %bitcast.18, bf16[24,64,768]{2,1,0:T(8,128)(2,1)} %bitcast.19), custom_call_target="tpu_custom_call" | custom-call | bytes 1048576 | tf_op jit(solution)/shard_map/pallas_call | solution.py:253
  54.2 36.6 %collective-permute-done.3.refs_3_ = bf16[24,64,768]{2,1,0:T(8,128)(2,1)S(1)} collective-permute-done((bf16[24,64,768]{2,1,0:T(8,128)(2,1)}, bf16[24,64,768]{2,1,0:T(8,128)(2,1)S(1)}, u32[]{:S(2)}, u32[]{:S(2)}) %collective-permute-start.3) | collective-permute-done | bytes 2359328 | tf_op jit(solution)/shard_map/ppermute | solution.py:430
  90.7 3.1 %collective-permute-done.2.refs_2_ = bf16[24,64,768]{2,1,0:T(8,128)(2,1)} collective-permute-done((bf16[24,64,768]{2,1,0:T(8,128)(2,1)}, bf16[24,64,768]{2,1,0:T(8,128)(2,1)}, u32[]{:S(2)}, u32[]{:S(2)}) %collective-permute-start.2) | collective-permute-done | bytes 2359328 | tf_op jit(solution)/shard_map/ppermute | solution.py:430
  93.9 8.6 %shard_map.75 = (bf16[24,64,768]{2,1,0:T(8,128)(2,1)}, bf16[24,64,768]{2,1,0:T(8,128)(2,1)}, bf16[24,64,768]{2,1,0:T(8,128)(2,1)}, bf16[24,64,768]{2,1,0:T(8,128)(2,1)}) custom-call(s32[16,6]{1,0:T(8,128)} %copy.29.index_ref, bf16[24,64,768]{2,1,0:T(8,128)(2,1)} %collective-permute-done.refs_0_, bf16[24,64,768]{2,1,0:T(8,128)(2,1)} %collective-permute-done.1.refs_1_, ...), custom_call_target="tpu_custom_call" | custom-call | bytes 1048576 | tf_op jit(solution)/shard_map/pallas_call | solution.py:165
  107.7 10.2 %shard_map.76 = (bf16[4,18,96,128]{3,2,1,0:T(8,128)(2,1)}, bf16[4,18,96,128]{3,2,1,0:T(8,128)(2,1)}) custom-call(s32[16,6]{1,0:T(8,128)} %copy.29.index_ref, s32[2]{0:T(128)} %pad_add_fusion.1.here_ref, bf16[2,768,768]{2,1,0:T(8,128)(2,1)} %bitcast.20, ...), custom_call_target="tpu_custom_call", output_to_operand_aliasing={{0}: (8, {}), {1}: (9, {})} | custom-call | bytes 1048576 | tf_op jit(solution)/shard_map/pallas_call | solution.py:253
  117.8 4.0 %collective-permute-start.4 = (bf16[4,18,96,128]{3,2,1,0:T(8,128)(2,1)}, bf16[4,18,96,128]{3,2,1,0:T(8,128)(2,1)S(1)}, u32[]{:S(2)}, u32[]{:S(2)}) collective-permute-start(bf16[4,18,96,128]{3,2,1,0:T(8,128)(2,1)} %get-tuple-element.28), channel_id=1, source_target_pairs={{0,1},{1,0},{2,3},{3,2},{4,5},{5,4},{6,7},{7,6},{8,9},{9,8},{10,11... | collective-permute-start | bytes 5308424 | tf_op jit(solution)/shard_map/ppermute | solution.py:447
  121.8 3.5 %collective-permute-done.4.came_ref = bf16[4,18,96,128]{3,2,1,0:T(8,128)(2,1)S(1)} collective-permute-done((bf16[4,18,96,128]{3,2,1,0:T(8,128)(2,1)}, bf16[4,18,96,128]{3,2,1,0:T(8,128)(2,1)S(1)}, u32[]{:S(2)}, u32[]{:S(2)}) %collective-permute-start.4) | collective-permute-done | bytes 1769504 | tf_op jit(solution)/shard_map/ppermute | solution.py:447
  126.6 5.1 %shard_map.77.refs_4_ = bf16[4,18,96,128]{3,2,1,0:T(8,128)(2,1)} custom-call(bf16[4,18,96,128]{3,2,1,0:T(8,128)(2,1)} %get-tuple-element.27.keep_ref, bf16[4,18,96,128]{3,2,1,0:T(8,128)(2,1)} %copy-done.3), custom_call_target="tpu_custom_call" | custom-call | bytes 1048576 | tf_op jit(solution)/shard_map/pallas_call | solution.py:287
  131.7 4.4 %all-to-all-start.1 = ((bf16[4,18,96,128]{3,2,1,0:T(8,128)(2,1)}), bf16[4,18,96,128]{3,2,1,0:T(8,128)(2,1)}, u32[]{:S(2)}, u32[]{:S(2)}) async-start(bf16[4,18,96,128]{3,2,1,0:T(8,128)(2,1)} %shard_map.77.refs_4_), calls=%async_computation.1 | async-start | bytes 3538944 | tf_op jit(solution)/shard_map/all_to_all | solution.py:458
  136.1 16.5 %collective-permute-done.6.refs_1_ = bf16[24,64,768]{2,1,0:T(8,128)(2,1)} collective-permute-done((bf16[24,64,768]{2,1,0:T(8,128)(2,1)}, bf16[24,64,768]{2,1,0:T(8,128)(2,1)}, u32[]{:S(2)}, u32[]{:S(2)}) %collective-permute-start.6) | collective-permute-done | bytes 2359328 | tf_op jit(solution)/shard_map/ppermute | solution.py:430
  157.8 6.9 %shard_map.79 = (bf16[12,64,768]{2,1,0:T(8,128)(2,1)}, bf16[12,64,768]{2,1,0:T(8,128)(2,1)}, bf16[12,64,768]{2,1,0:T(8,128)(2,1)}, bf16[12,64,768]{2,1,0:T(8,128)(2,1)}, bf16[6,64,768]{2,1,0:T(8,128)(2,1)}) custom-call(s32[16,6]{1,0:T(8,128)} %copy.29.index_ref, bf16[24,64,768]{2,1,0:T(8,128)(2,1)} %collective-permute-done.5.refs_0_, ...), custom_call_target="tpu_custom_call" | custom-call | bytes 1048576 | tf_op jit(solution)/shard_map/pallas_call | solution.py:165
  170.1 13.2 %shard_map.80.refs_1_ = bf16[8,18,96,128]{3,2,1,0:T(8,128)(2,1)} custom-call(s32[16,6]{1,0:T(8,128)} %copy.29.index_ref, s32[2]{0:T(128)} %pad_add_fusion.1.here_ref, bf16[2,768,768]{2,1,0:T(8,128)(2,1)} %bitcast.21, bf16[24,64,768]{2,1,0:T(8,128)(2,1)} %collective-permute-done.5.refs_0_, bf16[24,64,768]{2,1,0:T(8,128)(2,1)} %collective-permute-done.6.refs_1_, ...), custom_call_target="tpu_custom_call" | custom-call | bytes 1048576 | tf_op jit(solution)/shard_map/pallas_call | solution.py:253
  186.2 9.9 %all-to-all-start.2 = ((bf16[8,18,96,128]{3,2,1,0:T(8,128)(2,1)}), bf16[8,18,96,128]{3,2,1,0:T(8,128)(2,1)}, u32[]{:S(2)}, u32[]{:S(2)}) async-start(bf16[8,18,96,128]{3,2,1,0:T(8,128)(2,1)} %shard_map.80.refs_1_), calls=%async_computation.2 | async-start | bytes 7077888 | tf_op jit(solution)/shard_map/all_to_all | solution.py:493
  196.2 7.3 %collective-permute-done.14.refs_5_ = bf16[6,64,768]{2,1,0:T(8,128)(2,1)} collective-permute-done((bf16[6,64,768]{2,1,0:T(8,128)(2,1)}, bf16[6,64,768]{2,1,0:T(8,128)(2,1)}, u32[]{:S(2)}, u32[]{:S(2)}) %collective-permute-start.14) | collective-permute-done | bytes 589856 | tf_op jit(solution)/shard_map/ppermute | solution.py:430
  207.0 11.6 %shard_map.83 = (bf16[4,15,96,128]{3,2,1,0:T(8,128)(2,1)}, bf16[4,15,96,128]{3,2,1,0:T(8,128)(2,1)}) custom-call(s32[16,6]{1,0:T(8,128)} %copy.29.index_ref, s32[2]{0:T(128)} %pad_add_fusion.1.here_ref, bf16[2,768,768]{2,1,0:T(8,128)(2,1)} %bitcast.22, bf16[12,64,768]{2,1,0:T(8,128)(2,1)} %collective-permute-done.9.refs_0_, bf16[12,64,768]{2,1,0:T(8,128)(2,1)} %copy-done.13, ...), custom_call_target="tpu_custom_call" | custom-call | flops 999999995904 | bytes 1048576 | tf_op jit(solution)/shard_map/pallas_call | solution.py:253
  218.7 3.6 %collective-permute-start.15 = (bf16[4,15,96,128]{3,2,1,0:T(8,128)(2,1)}, bf16[4,15,96,128]{3,2,1,0:T(8,128)(2,1)S(1)}, u32[]{:S(2)}, u32[]{:S(2)}) collective-permute-start(bf16[4,15,96,128]{3,2,1,0:T(8,128)(2,1)} %get-tuple-element.38), channel_id=1, source_target_pairs={{0,1},{1,0},{2,3},{3,2},{4,5},{5,4},{6,7},{7,6},{8,9},{9,8},{10,11... | collective-permute-start | bytes 4423688 | tf_op jit(solution)/shard_map/ppermute | solution.py:447
  226.5 3.8 %shard_map.84 = (f32[15,96,128]{2,1,0:T(8,128)}, bf16[15,96,128]{2,1,0:T(8,128)(2,1)}, bf16[15,96,128]{2,1,0:T(8,128)(2,1)}, bf16[15,96,128]{2,1,0:T(8,128)(2,1)}) custom-call(s32[2]{0:T(128)} %pad_add_fusion.1.here_ref, bf16[4,15,96,128]{3,2,1,0:T(8,128)(2,1)} %get-tuple-element.37.keep_ref, bf16[4,15,96,128]{3,2,1,0:T(8,128)(2,1)} %copy-done.4), custom_call_target="tpu_custom_call" | custom-call | bytes 1048576 | tf_op jit(solution)/shard_map/pallas_call | solution.py:304
  237.4 4.7 %shard_map.78.refs_0_ = bf16[2,18,96,128]{3,2,1,0:T(8,128)(2,1)} custom-call(bf16[4,18,96,128]{3,2,1,0:T(8,128)(2,1)} %all-to-all-done.1.given_ref.refs_6_), custom_call_target="tpu_custom_call" | custom-call | bytes 1048576 | tf_op jit(solution)/shard_map/pallas_call | solution.py:327
  242.0 5.2 %shard_map.81.refs_1_ = bf16[2,18,96,128]{3,2,1,0:T(8,128)(2,1)} custom-call(bf16[8,18,96,128]{3,2,1,0:T(8,128)(2,1)} %all-to-all-done.2.given_ref), custom_call_target="tpu_custom_call" | custom-call | bytes 1048576 | tf_op jit(solution)/shard_map/pallas_call | solution.py:327
  247.2 6.9 %collective-permute-done.17.refs_4_ = bf16[15,96,128]{2,1,0:T(8,128)(2,1)S(1)} collective-permute-done((bf16[15,96,128]{2,1,0:T(8,128)(2,1)}, bf16[15,96,128]{2,1,0:T(8,128)(2,1)S(1)}, u32[]{:S(2)}, u32[]{:S(2)}) %collective-permute-start.17) | collective-permute-done | bytes 368672 | tf_op jit(solution)/shard_map/ppermute | solution.py:453
  255.0 5.6 %shard_map.85 = bf16[96,12288]{1,0:T(8,128)(2,1)} custom-call(s32[96]{0:T(128)} %slice.12.left_ref, s32[96]{0:T(128)} %slice.13.right_ref, s32[2]{0:T(128)} %pad_add_fusion.1.here_ref, bf16[2,18,96,128]{3,2,1,0:T(8,128)(2,1)} %shard_map.78.refs_0_, bf16[2,18,96,128]{3,2,1,0:T(8,128)(2,1)} %shard_map.81.refs_1_, f32[15,96,128]{2,1,0:T(8,128)} %get-tuple-element.39.refs_2_, ...), custom_call_target="tpu_custom_call" | custom-call | tf_op jit(solution)/shard_map/pallas_call | solution.py:388
  (97 shorter events, 46.5 us)
Async XLA Ops:
  1.8 21.4 %all-to-all-start = ((bf16[16,32,768]{2,1,0:T(8,128)(2,1)}), bf16[16,32,768]{2,1,0:T(8,128)(2,1)S(1)}, u32[]{:S(2)}, u32[]{:S(2)}) async-start(bf16[16,32,768]{2,1,0:T(8,128)(2,1)} %broadcast_in_dim.54), calls=%async_computation | async-start | bytes 1572864 | tf_op jit(solution)/shard_map/all_to_all | solution.py:408
  11.2 31.5 %copy-start.9 = (s32[192,4]{0,1:T(4,128)S(1)}, s32[192,4]{0,1:T(4,128)}, u32[]{:S(2)}) copy-start(s32[192,4]{0,1:T(4,128)} %param.10) | copy-start | bytes 9220
  39.7 51.0 %collective-permute-start.3 = (bf16[24,64,768]{2,1,0:T(8,128)(2,1)}, bf16[24,64,768]{2,1,0:T(8,128)(2,1)S(1)}, u32[]{:S(2)}, u32[]{:S(2)}) collective-permute-start(bf16[24,64,768]{2,1,0:T(8,128)(2,1)} %bitcast.14), channel_id=1, source_target_pairs={{0,24},{8,0},{16,8},{24,16},{32,56},{40,32},{48,40},{56,48},{64,88... | collective-permute-start | bytes 7077896 | tf_op jit(solution)/shard_map/ppermute | solution.py:430
  41.2 52.6 %collective-permute-start.2 = (bf16[24,64,768]{2,1,0:T(8,128)(2,1)}, bf16[24,64,768]{2,1,0:T(8,128)(2,1)}, u32[]{:S(2)}, u32[]{:S(2)}) collective-permute-start(bf16[24,64,768]{2,1,0:T(8,128)(2,1)} %bitcast.15), channel_id=1, source_target_pairs={{0,8},{8,16},{16,24},{24,0},{32,40},{40,48},{48,56},{56,32},{64,72... | collective-permute-start | bytes 7077896 | tf_op jit(solution)/shard_map/ppermute | solution.py:430
  41.2 52.6 %collective-permute-start.1 = (bf16[24,64,768]{2,1,0:T(8,128)(2,1)}, bf16[24,64,768]{2,1,0:T(8,128)(2,1)}, u32[]{:S(2)}, u32[]{:S(2)}) collective-permute-start(bf16[24,64,768]{2,1,0:T(8,128)(2,1)} %bitcast.16), channel_id=1, source_target_pairs={{0,96},{8,104},{16,112},{24,120},{32,0},{40,8},{48,16},{56,24},{64... | collective-permute-start | bytes 7077896 | tf_op jit(solution)/shard_map/ppermute | solution.py:430
  42.4 51.5 %collective-permute-start = (bf16[24,64,768]{2,1,0:T(8,128)(2,1)}, bf16[24,64,768]{2,1,0:T(8,128)(2,1)}, u32[]{:S(2)}, u32[]{:S(2)}) collective-permute-start(bf16[24,64,768]{2,1,0:T(8,128)(2,1)} %bitcast.17), channel_id=1, source_target_pairs={{0,32},{8,40},{16,48},{24,56},{32,64},{40,72},{48,80},{56,88},{64,... | collective-permute-start | bytes 7077896 | tf_op jit(solution)/shard_map/ppermute | solution.py:430
  102.5 50.1 %collective-permute-start.6 = (bf16[24,64,768]{2,1,0:T(8,128)(2,1)}, bf16[24,64,768]{2,1,0:T(8,128)(2,1)}, u32[]{:S(2)}, u32[]{:S(2)}) collective-permute-start(bf16[24,64,768]{2,1,0:T(8,128)(2,1)} %get-tuple-element.29), channel_id=1, source_target_pairs={{0,96},{8,104},{16,112},{24,120},{32,0},{40,8},{48,16},{56,24},{64... | collective-permute-start | bytes 7077896 | tf_op jit(solution)/shard_map/ppermute | solution.py:430
  104.1 51.7 %collective-permute-start.7 = (bf16[24,64,768]{2,1,0:T(8,128)(2,1)}, bf16[24,64,768]{2,1,0:T(8,128)(2,1)}, u32[]{:S(2)}, u32[]{:S(2)}) collective-permute-start(bf16[24,64,768]{2,1,0:T(8,128)(2,1)} %get-tuple-element.30), channel_id=1, source_target_pairs={{0,8},{8,16},{16,24},{24,0},{32,40},{40,48},{48,56},{56,32},{64,72... | collective-permute-start | bytes 7077896 | tf_op jit(solution)/shard_map/ppermute | solution.py:430
  104.1 51.7 %collective-permute-start.8 = (bf16[24,64,768]{2,1,0:T(8,128)(2,1)}, bf16[24,64,768]{2,1,0:T(8,128)(2,1)S(1)}, u32[]{:S(2)}, u32[]{:S(2)}) collective-permute-start(bf16[24,64,768]{2,1,0:T(8,128)(2,1)} %get-tuple-element.31), channel_id=1, source_target_pairs={{0,24},{8,0},{16,8},{24,16},{32,56},{40,32},{48,40},{56,48},{64,88... | collective-permute-start | bytes 7077896 | tf_op jit(solution)/shard_map/ppermute | solution.py:430
  106.7 51.1 %collective-permute-start.5 = (bf16[24,64,768]{2,1,0:T(8,128)(2,1)}, bf16[24,64,768]{2,1,0:T(8,128)(2,1)}, u32[]{:S(2)}, u32[]{:S(2)}) collective-permute-start(bf16[24,64,768]{2,1,0:T(8,128)(2,1)} %get-tuple-element.25.refs_4_), channel_id=1, source_target_pairs={{0,32},{8,40},{16,48},{24,56},{32,64},{40,72},{48,80},{56,88},{64,... | collective-permute-start | bytes 7077896 | tf_op jit(solution)/shard_map/ppermute | solution.py:430
  117.8 7.5 %collective-permute-start.4 = (bf16[4,18,96,128]{3,2,1,0:T(8,128)(2,1)}, bf16[4,18,96,128]{3,2,1,0:T(8,128)(2,1)S(1)}, u32[]{:S(2)}, u32[]{:S(2)}) collective-permute-start(bf16[4,18,96,128]{3,2,1,0:T(8,128)(2,1)} %get-tuple-element.28), channel_id=1, source_target_pairs={{0,1},{1,0},{2,3},{3,2},{4,5},{5,4},{6,7},{7,6},{8,9},{9,8},{10,11... | collective-permute-start | bytes 5308424 | tf_op jit(solution)/shard_map/ppermute | solution.py:447
  131.7 54.5 %all-to-all-start.1 = ((bf16[4,18,96,128]{3,2,1,0:T(8,128)(2,1)}), bf16[4,18,96,128]{3,2,1,0:T(8,128)(2,1)}, u32[]{:S(2)}, u32[]{:S(2)}) async-start(bf16[4,18,96,128]{3,2,1,0:T(8,128)(2,1)} %shard_map.77.refs_4_), calls=%async_computation.1 | async-start | bytes 3538944 | tf_op jit(solution)/shard_map/all_to_all | solution.py:458
  164.8 21.3 %collective-permute-start.13 = (bf16[6,64,768]{2,1,0:T(8,128)(2,1)}, bf16[6,64,768]{2,1,0:T(8,128)(2,1)}, u32[]{:S(2)}, u32[]{:S(2)}) collective-permute-start(bf16[6,64,768]{2,1,0:T(8,128)(2,1)} %get-tuple-element.36), channel_id=1, source_target_pairs={{0,16},{8,24},{16,0},{24,8},{32,48},{40,56},{48,32},{56,40},{64,80... | collective-permute-start | bytes 1769480 | tf_op jit(solution)/shard_map/ppermute | solution.py:430
  165.9 39.3 %collective-permute-start.10 = (bf16[12,64,768]{2,1,0:T(8,128)(2,1)}, bf16[12,64,768]{2,1,0:T(8,128)(2,1)S(1)}, u32[]{:S(2)}, u32[]{:S(2)}) collective-permute-start(bf16[12,64,768]{2,1,0:T(8,128)(2,1)} %get-tuple-element.33), channel_id=1, source_target_pairs={{0,24},{8,0},{16,8},{24,16},{32,56},{40,32},{48,40},{56,48},{64,88... | collective-permute-start | bytes 3538952 | tf_op jit(solution)/shard_map/ppermute | solution.py:430
  166.7 38.6 %collective-permute-start.11 = (bf16[12,64,768]{2,1,0:T(8,128)(2,1)}, bf16[12,64,768]{2,1,0:T(8,128)(2,1)S(1)}, u32[]{:S(2)}, u32[]{:S(2)}) collective-permute-start(bf16[12,64,768]{2,1,0:T(8,128)(2,1)} %get-tuple-element.34), channel_id=1, source_target_pairs={{0,32},{8,40},{16,48},{24,56},{32,64},{40,72},{48,80},{56,88},{64,... | collective-permute-start | bytes 3538952 | tf_op jit(solution)/shard_map/ppermute | solution.py:430
  168.1 37.2 %collective-permute-start.12 = (bf16[12,64,768]{2,1,0:T(8,128)(2,1)}, bf16[12,64,768]{2,1,0:T(8,128)(2,1)S(1)}, u32[]{:S(2)}, u32[]{:S(2)}) collective-permute-start(bf16[12,64,768]{2,1,0:T(8,128)(2,1)} %get-tuple-element.35), channel_id=1, source_target_pairs={{0,96},{8,104},{16,112},{24,120},{32,0},{40,8},{48,16},{56,24},{64... | collective-permute-start | bytes 3538952 | tf_op jit(solution)/shard_map/ppermute | solution.py:430
  169.3 37.2 %collective-permute-start.9 = (bf16[12,64,768]{2,1,0:T(8,128)(2,1)}, bf16[12,64,768]{2,1,0:T(8,128)(2,1)}, u32[]{:S(2)}, u32[]{:S(2)}) collective-permute-start(bf16[12,64,768]{2,1,0:T(8,128)(2,1)} %get-tuple-element.32.refs_4_), channel_id=1, source_target_pairs={{0,8},{8,16},{16,24},{24,0},{32,40},{40,48},{48,56},{56,32},{64,72... | collective-permute-start | bytes 3538952 | tf_op jit(solution)/shard_map/ppermute | solution.py:430
  186.0 17.4 %collective-permute-start.14 = (bf16[6,64,768]{2,1,0:T(8,128)(2,1)}, bf16[6,64,768]{2,1,0:T(8,128)(2,1)}, u32[]{:S(2)}, u32[]{:S(2)}) collective-permute-start(bf16[6,64,768]{2,1,0:T(8,128)(2,1)} %shard_map.82), channel_id=1, source_target_pairs={{0,64},{8,72},{16,80},{24,88},{32,96},{40,104},{48,112},{56,120},{... | collective-permute-start | bytes 1769480 | tf_op jit(solution)/shard_map/ppermute | solution.py:430
  186.2 55.8 %all-to-all-start.2 = ((bf16[8,18,96,128]{3,2,1,0:T(8,128)(2,1)}), bf16[8,18,96,128]{3,2,1,0:T(8,128)(2,1)}, u32[]{:S(2)}, u32[]{:S(2)}) async-start(bf16[8,18,96,128]{3,2,1,0:T(8,128)(2,1)} %shard_map.80.refs_1_), calls=%async_computation.2 | async-start | bytes 7077888 | tf_op jit(solution)/shard_map/all_to_all | solution.py:493
  218.7 17.2 %copy-start.11 = (pred[192]{0:T(512)(128)(4,1)S(1)}, pred[192]{0:T(512)(128)(4,1)}, u32[]{:S(2)}) copy-start(pred[192]{0:T(512)(128)(4,1)} %copy-done.10) | copy-start | bytes 580
  218.7 6.7 %collective-permute-start.15 = (bf16[4,15,96,128]{3,2,1,0:T(8,128)(2,1)}, bf16[4,15,96,128]{3,2,1,0:T(8,128)(2,1)S(1)}, u32[]{:S(2)}, u32[]{:S(2)}) collective-permute-start(bf16[4,15,96,128]{3,2,1,0:T(8,128)(2,1)} %get-tuple-element.38), channel_id=1, source_target_pairs={{0,1},{1,0},{2,3},{3,2},{4,5},{5,4},{6,7},{7,6},{8,9},{9,8},{10,11... | collective-permute-start | bytes 4423688 | tf_op jit(solution)/shard_map/ppermute | solution.py:447
  230.3 16.9 %collective-permute-start.16 = (bf16[15,96,128]{2,1,0:T(8,128)(2,1)}, bf16[15,96,128]{2,1,0:T(8,128)(2,1)S(1)}, u32[]{:S(2)}, u32[]{:S(2)}) collective-permute-start(bf16[15,96,128]{2,1,0:T(8,128)(2,1)} %get-tuple-element.40), channel_id=1, source_target_pairs={{0,4},{1,5},{2,6},{3,7},{4,0},{5,1},{6,2},{7,3},{8,12},{9,13},{10,... | collective-permute-start | bytes 1105928 | tf_op jit(solution)/shard_map/ppermute | solution.py:453
  233.0 21.1 %collective-permute-start.17 = (bf16[15,96,128]{2,1,0:T(8,128)(2,1)}, bf16[15,96,128]{2,1,0:T(8,128)(2,1)S(1)}, u32[]{:S(2)}, u32[]{:S(2)}) collective-permute-start(bf16[15,96,128]{2,1,0:T(8,128)(2,1)} %get-tuple-element.41), channel_id=1, source_target_pairs={{0,2},{1,3},{2,4},{3,5},{4,6},{5,7},{6,0},{7,1},{8,10},{9,11},{10,... | collective-permute-start | bytes 1105928 | tf_op jit(solution)/shard_map/ppermute | solution.py:453
  233.3 20.8 %collective-permute-start.18 = (bf16[15,96,128]{2,1,0:T(8,128)(2,1)}, bf16[15,96,128]{2,1,0:T(8,128)(2,1)S(1)}, u32[]{:S(2)}, u32[]{:S(2)}) collective-permute-start(bf16[15,96,128]{2,1,0:T(8,128)(2,1)} %get-tuple-element.42), channel_id=1, source_target_pairs={{0,6},{1,7},{2,0},{3,1},{4,2},{5,3},{6,4},{7,5},{8,14},{9,15},{10,... | collective-permute-start | bytes 1105928 | tf_op jit(solution)/shard_map/ppermute | solution.py:453
  (14 other events, 49.5 us)

commit v4 on v3

--- a/solution.py
+++ b/solution.py
@@ -174,7 +174,7 @@
     )(index, *operands)
 
 
-def product_kernel(scale, jobs, n_in, split, index_ref, here_ref, own_ref, *refs):
+def product_kernel(scale, jobs, per, n_in, split, index_ref, here_ref, own_ref, *refs):
     ins, outs = refs[:n_in], refs[n_in:-4]
     left, side, own_sems, sems = refs[-4:]
     step = pl.program_id(0)
@@ -191,16 +191,19 @@
                 made.append((given, left.at[half, pl.ds(n * PIECE, PIECE)], own_sems.at[half, n]))
         return [pltpu.make_async_copy(*copy) for copy in made]
 
-    def copies(job, slot):
+    def copies(group, slot):
         made = []
-        for half, (source, row, first) in enumerate(jobs[job]):
-            if row is None:
-                given = ins[source].at[pl.ds(first, CAP)]
-                made.append((given, side.at[slot, half], sems.at[slot, half, 0]))
-                continue
-            for s in range(CAP):
-                given = ins[source].at[first + index_ref[row, s]]
-                made.append((given, side.at[slot, half, s], sems.at[slot, half, s]))
+        for n in range(per):
+            for half, (source, row, first) in enumerate(jobs[group * per + n]):
+                at = n * CAP
+                if row is None:
+                    given = ins[source].at[pl.ds(first, CAP)]
+                    to = side.at[slot, half, pl.ds(at, CAP)]
+                    made.append((given, to, sems.at[slot, half, at]))
+                    continue
+                for s in range(at, at + CAP):
+                    given = ins[source].at[first + index_ref[row, s - at]]
+                    made.append((given, side.at[slot, half, s], sems.at[slot, half, s]))
         return [pltpu.make_async_copy(*copy) for copy in made]
 
     def begin(job):
@@ -215,25 +218,25 @@
         for copy in own_copies():
             copy.wait()
 
-    for job in range(len(jobs)):
+    for job in range(len(jobs) // per):
 
         @pl.when(step == job)
         def _(job=job):
-            if job + 1 < len(jobs):
+            if job + 1 < len(jobs) // per:
                 begin(job + 1)
             for copy in copies(job, job % 2):
                 copy.wait()
 
     slot = lax.rem(step, 2)
     last = (((1,), (1,)), ((), ()))
-    side_a = side[slot, 0].reshape(CAP * BS, HALF)
-    side_b = side[slot, 1].reshape(CAP * BS, HALF)
+    side_a = side[slot, 0].reshape(per * CAP * BS, HALF)
+    side_b = side[slot, 1].reshape(per * CAP * BS, HALF)
     total = lax.dot_general(left[0], side_a, last, preferred_element_type=jnp.float32)
     total += lax.dot_general(left[1], side_b, last, preferred_element_type=jnp.float32)
     total = (total * scale).astype(jnp.bfloat16)
     pieces = FIT // len(outs)
     for n in range(FIT):
-        for t in range(TILES):
+        for t in range(per * TILES):
             part = total[n * PIECE : (n + 1) * PIECE, t * 128 : (t + 1) * 128]
             outs[n // pieces][n % pieces, t] = part
 
@@ -249,18 +252,20 @@
     pieces = FIT // 2 if split else FIT
     shape = (pieces, count, PIECE, 128)
     kinds = [jnp.bfloat16] * (2 if split else 1)
-    out = pl.BlockSpec((pieces, TILES, PIECE, 128), lambda j: (0, tile // TILES + j, 0, 0))
-    return pl.pallas_call(
-        functools.partial(product_kernel, scale, jobs, len(sources) + len(extra), split),
-        grid=(len(jobs),),
+    per = 2 if len(jobs) % 2 == 0 else 1
+    block = per * TILES
+    out = pl.BlockSpec((pieces, block, PIECE, 128), lambda j: (0, tile // block + j, 0, 0))
+    return pl.pallas_call(
+        functools.partial(product_kernel, scale, jobs, per, len(sources) + len(extra), split),
+        grid=(len(jobs) // per,),
         in_specs=[smem, smem] + [anywhere] * len(given),
         out_specs=[out] * len(kinds),
         out_shape=[jax.ShapeDtypeStruct(shape, kind) for kind in kinds],
         scratch_shapes=[
             pltpu.VMEM((2, ROWS, HALF), jnp.bfloat16),
-            pltpu.VMEM((2, 2, CAP, BS, HALF), jnp.bfloat16),
+            pltpu.VMEM((2, 2, per * CAP, BS, HALF), jnp.bfloat16),
             pltpu.SemaphoreType.DMA((2, FIT)),
-            pltpu.SemaphoreType.DMA((2, 2, CAP)),
+            pltpu.SemaphoreType.DMA((2, 2, per * CAP)),
         ],
         input_output_aliases={len(operands) - len(buffers) + n: n for n in range(len(buffers))},
         compiler_params=pltpu.CompilerParams(vmem_limit_bytes=58 * MIB),

time: 262 us -> 261 us (level)
    pallas_call x4, Pallas kernels: 41.9 us -> 39.1 us  [product(): pl.pallas_call(functools.partial(product_kernel, scale, jobs, per, len(so...]
  transfers between devices with their start and end apart: 22 -> 22, of which waited for: 12 -> 12; matrix products, arithmetic and copies ran while one was open for 3% -> 3% of each run, Pallas kernels for 27% -> 26%
where the time goes in v4:
time: 261 us; the launch traced here: 259 us
  Pallas kernels  97.4 us (37%)
  waiting for transfers between devices  96.9 us (37%)
  starting transfers between devices  50 us (19%)
  local copies, waits for them, and re-layouts  11.4 us (4%)
  other arithmetic  3.09 us (1%)
    ppermute x14, waiting for transfers between devices, send(): return lax.ppermute(payload, 'atom', route)  73.9 us
    pallas_call x4, Pallas kernels, product(): pl.pallas_call(functools.partial(product_kernel, scale, jobs, per, len(so...  39.1 us
    pallas_call x3, Pallas kernels, pack(): pl.pallas_call(functools.partial(pack_kernel, jobs, len(operands)), in_sp...  18.3 us
    pallas_call x1, Pallas kernels, fit_rows(): pl.pallas_call(fit_kernel, grid=(NBD // 2,), in_specs=[pl.BlockSpec(memor...  15.7 us
    ppermute x14, starting transfers between devices, send(): return lax.ppermute(payload, 'atom', route)  13.9 us
    all_to_all x1, waiting for transfers between devices, per_device(): everyone = lax.all_to_all(everyone, 'atom', 0, 0, tiled=True)  12 us
    all_to_all x1, starting transfers between devices, per_device(): second_came = lax.all_to_all(partial, 'fit', 0, 0, tiled=True)  9.95 us
    pallas_call x2, Pallas kernels, sum_pieces(): pl.pallas_call(sum_kernel, grid=(count // TILES,), in_specs=[pl.BlockSpec...  9.82 us
  transfers between devices with their start and end apart: 22, of which 12 were waited for; matrix products, arithmetic and copies ran while one was open for 3% of the time, Pallas kernels for 26%

profile of v4, /device:TPU:1, one launch (start us, length us, event | category | flops | bytes accessed | tf_op | source)
XLA Modules:
  0.0 259.2 jit_solution(4804677136839421569)
XLA Ops:
  1.8 8.6 %all-to-all-start = ((bf16[16,32,768]{2,1,0:T(8,128)(2,1)}), bf16[16,32,768]{2,1,0:T(8,128)(2,1)S(1)}, u32[]{:S(2)}, u32[]{:S(2)}) async-start(bf16[16,32,768]{2,1,0:T(8,128)(2,1)} %broadcast_in_dim.54), calls=%async_computation | async-start | bytes 1572864 | tf_op jit(solution)/shard_map/all_to_all | solution.py:413
  11.2 12.0 %all-to-all-done.coeff_ref = bf16[16,32,768]{2,1,0:T(8,128)(2,1)S(1)} async-done(((bf16[16,32,768]{2,1,0:T(8,128)(2,1)}), bf16[16,32,768]{2,1,0:T(8,128)(2,1)S(1)}, u32[]{:S(2)}, u32[]{:S(2)}) %all-to-all-start) | async-done | bytes 786464 | tf_op jit(solution)/shard_map/all_to_all | solution.py:413
  24.0 15.7 %shard_map.73 = bf16[2,12,64,768]{3,2,1,0:T(8,128)(2,1)} custom-call(s32[3,48]{1,0:T(4,128)} %pad_add_fusion.where_ref, bf16[12,4,48,4096]{3,2,1,0:T(8,128)(2,1)} %tile_ref.1, bf16[16,32,768]{2,1,0:T(8,128)(2,1)} %copy-done.2, bf16[4,128,256]{2,1,0:T(8,128)(2,1)} %constant.70.clone.spread_ref), custom_call_target="tpu_custom_call" | custom-call | flops 1073741824 | bytes 20971520 | tf_op jit(solution)/shard_map/pallas_call | solution.py:121
  47.2 6.9 %shard_map.74 = (bf16[4,18,96,128]{3,2,1,0:T(8,128)(2,1)}, bf16[4,18,96,128]{3,2,1,0:T(8,128)(2,1)}) custom-call(s32[16,6]{1,0:T(8,128)} %copy.29.index_ref, s32[2]{0:T(128)} %pad_add_fusion.1.here_ref, bf16[2,768,768]{2,1,0:T(8,128)(2,1)} %bitcast.18, bf16[24,64,768]{2,1,0:T(8,128)(2,1)} %bitcast.19), custom_call_target="tpu_custom_call" | custom-call | bytes 1048576 | tf_op jit(solution)/shard_map/pallas_call | solution.py:258
  54.1 36.6 %collective-permute-done.3.refs_3_ = bf16[24,64,768]{2,1,0:T(8,128)(2,1)S(1)} collective-permute-done((bf16[24,64,768]{2,1,0:T(8,128)(2,1)}, bf16[24,64,768]{2,1,0:T(8,128)(2,1)S(1)}, u32[]{:S(2)}, u32[]{:S(2)}) %collective-permute-start.3) | collective-permute-done | bytes 2359328 | tf_op jit(solution)/shard_map/ppermute | solution.py:435
  93.9 8.7 %shard_map.75 = (bf16[24,64,768]{2,1,0:T(8,128)(2,1)}, bf16[24,64,768]{2,1,0:T(8,128)(2,1)}, bf16[24,64,768]{2,1,0:T(8,128)(2,1)}, bf16[24,64,768]{2,1,0:T(8,128)(2,1)}) custom-call(s32[16,6]{1,0:T(8,128)} %copy.29.index_ref, bf16[24,64,768]{2,1,0:T(8,128)(2,1)} %collective-permute-done.refs_0_, bf16[24,64,768]{2,1,0:T(8,128)(2,1)} %collective-permute-done.1.refs_1_, ...), custom_call_target="tpu_custom_call" | custom-call | bytes 1048576 | tf_op jit(solution)/shard_map/pallas_call | solution.py:165
  107.7 9.1 %shard_map.76 = (bf16[4,18,96,128]{3,2,1,0:T(8,128)(2,1)}, bf16[4,18,96,128]{3,2,1,0:T(8,128)(2,1)}) custom-call(s32[16,6]{1,0:T(8,128)} %copy.29.index_ref, s32[2]{0:T(128)} %pad_add_fusion.1.here_ref, bf16[2,768,768]{2,1,0:T(8,128)(2,1)} %bitcast.20, ...), custom_call_target="tpu_custom_call", output_to_operand_aliasing={{0}: (8, {}), {1}: (9, {})} | custom-call | bytes 1048576 | tf_op jit(solution)/shard_map/pallas_call | solution.py:258
  116.8 4.1 %collective-permute-start.4 = (bf16[4,18,96,128]{3,2,1,0:T(8,128)(2,1)}, bf16[4,18,96,128]{3,2,1,0:T(8,128)(2,1)S(1)}, u32[]{:S(2)}, u32[]{:S(2)}) collective-permute-start(bf16[4,18,96,128]{3,2,1,0:T(8,128)(2,1)} %get-tuple-element.28), channel_id=1, source_target_pairs={{0,1},{1,0},{2,3},{3,2},{4,5},{5,4},{6,7},{7,6},{8,9},{9,8},{10,11... | collective-permute-start | bytes 5308424 | tf_op jit(solution)/shard_map/ppermute | solution.py:452
  120.9 3.5 %collective-permute-done.4.came_ref = bf16[4,18,96,128]{3,2,1,0:T(8,128)(2,1)S(1)} collective-permute-done((bf16[4,18,96,128]{3,2,1,0:T(8,128)(2,1)}, bf16[4,18,96,128]{3,2,1,0:T(8,128)(2,1)S(1)}, u32[]{:S(2)}, u32[]{:S(2)}) %collective-permute-start.4) | collective-permute-done | bytes 1769504 | tf_op jit(solution)/shard_map/ppermute | solution.py:452
  125.7 5.1 %shard_map.77.refs_4_ = bf16[4,18,96,128]{3,2,1,0:T(8,128)(2,1)} custom-call(bf16[4,18,96,128]{3,2,1,0:T(8,128)(2,1)} %get-tuple-element.27.keep_ref, bf16[4,18,96,128]{3,2,1,0:T(8,128)(2,1)} %copy-done.3), custom_call_target="tpu_custom_call" | custom-call | bytes 1048576 | tf_op jit(solution)/shard_map/pallas_call | solution.py:292
  130.8 4.4 %all-to-all-start.1 = ((bf16[4,18,96,128]{3,2,1,0:T(8,128)(2,1)}), bf16[4,18,96,128]{3,2,1,0:T(8,128)(2,1)}, u32[]{:S(2)}, u32[]{:S(2)}) async-start(bf16[4,18,96,128]{3,2,1,0:T(8,128)(2,1)} %shard_map.77.refs_4_), calls=%async_computation.1 | async-start | bytes 3538944 | tf_op jit(solution)/shard_map/all_to_all | solution.py:463
  135.2 17.4 %collective-permute-done.6.refs_1_ = bf16[24,64,768]{2,1,0:T(8,128)(2,1)} collective-permute-done((bf16[24,64,768]{2,1,0:T(8,128)(2,1)}, bf16[24,64,768]{2,1,0:T(8,128)(2,1)}, u32[]{:S(2)}, u32[]{:S(2)}) %collective-permute-start.6) | collective-permute-done | bytes 2359328 | tf_op jit(solution)/shard_map/ppermute | solution.py:435
  152.5 3.1 %collective-permute-done.7.refs_2_ = bf16[24,64,768]{2,1,0:T(8,128)(2,1)} collective-permute-done((bf16[24,64,768]{2,1,0:T(8,128)(2,1)}, bf16[24,64,768]{2,1,0:T(8,128)(2,1)}, u32[]{:S(2)}, u32[]{:S(2)}) %collective-permute-start.7) | collective-permute-done | bytes 2359328 | tf_op jit(solution)/shard_map/ppermute | solution.py:435
  157.8 6.8 %shard_map.79 = (bf16[12,64,768]{2,1,0:T(8,128)(2,1)}, bf16[12,64,768]{2,1,0:T(8,128)(2,1)}, bf16[12,64,768]{2,1,0:T(8,128)(2,1)}, bf16[12,64,768]{2,1,0:T(8,128)(2,1)}, bf16[6,64,768]{2,1,0:T(8,128)(2,1)}) custom-call(s32[16,6]{1,0:T(8,128)} %copy.29.index_ref, bf16[24,64,768]{2,1,0:T(8,128)(2,1)} %collective-permute-done.5.refs_0_, ...), custom_call_target="tpu_custom_call" | custom-call | bytes 1048576 | tf_op jit(solution)/shard_map/pallas_call | solution.py:165
  170.3 11.5 %shard_map.80.refs_1_ = bf16[8,18,96,128]{3,2,1,0:T(8,128)(2,1)} custom-call(s32[16,6]{1,0:T(8,128)} %copy.29.index_ref, s32[2]{0:T(128)} %pad_add_fusion.1.here_ref, bf16[2,768,768]{2,1,0:T(8,128)(2,1)} %bitcast.21, bf16[24,64,768]{2,1,0:T(8,128)(2,1)} %collective-permute-done.5.refs_0_, bf16[24,64,768]{2,1,0:T(8,128)(2,1)} %collective-permute-done.6.refs_1_, ...), custom_call_target="tpu_custom_call" | custom-call | bytes 1048576 | tf_op jit(solution)/shard_map/pallas_call | solution.py:258
  184.7 10.0 %all-to-all-start.2 = ((bf16[8,18,96,128]{3,2,1,0:T(8,128)(2,1)}), bf16[8,18,96,128]{3,2,1,0:T(8,128)(2,1)}, u32[]{:S(2)}, u32[]{:S(2)}) async-start(bf16[8,18,96,128]{3,2,1,0:T(8,128)(2,1)} %shard_map.80.refs_1_), calls=%async_computation.2 | async-start | bytes 7077888 | tf_op jit(solution)/shard_map/all_to_all | solution.py:498
  194.7 8.6 %collective-permute-done.14.refs_5_ = bf16[6,64,768]{2,1,0:T(8,128)(2,1)} collective-permute-done((bf16[6,64,768]{2,1,0:T(8,128)(2,1)}, bf16[6,64,768]{2,1,0:T(8,128)(2,1)}, u32[]{:S(2)}, u32[]{:S(2)}) %collective-permute-start.14) | collective-permute-done | bytes 589856 | tf_op jit(solution)/shard_map/ppermute | solution.py:435
  207.0 11.6 %shard_map.83 = (bf16[4,15,96,128]{3,2,1,0:T(8,128)(2,1)}, bf16[4,15,96,128]{3,2,1,0:T(8,128)(2,1)}) custom-call(s32[16,6]{1,0:T(8,128)} %copy.29.index_ref, s32[2]{0:T(128)} %pad_add_fusion.1.here_ref, bf16[2,768,768]{2,1,0:T(8,128)(2,1)} %bitcast.22, bf16[12,64,768]{2,1,0:T(8,128)(2,1)} %collective-permute-done.9.refs_0_, bf16[12,64,768]{2,1,0:T(8,128)(2,1)} %copy-done.13, ...), custom_call_target="tpu_custom_call" | custom-call | flops 999999995904 | bytes 1048576 | tf_op jit(solution)/shard_map/pallas_call | solution.py:258
  218.6 3.7 %collective-permute-start.15 = (bf16[4,15,96,128]{3,2,1,0:T(8,128)(2,1)}, bf16[4,15,96,128]{3,2,1,0:T(8,128)(2,1)S(1)}, u32[]{:S(2)}, u32[]{:S(2)}) collective-permute-start(bf16[4,15,96,128]{3,2,1,0:T(8,128)(2,1)} %get-tuple-element.38), channel_id=1, source_target_pairs={{0,1},{1,0},{2,3},{3,2},{4,5},{5,4},{6,7},{7,6},{8,9},{9,8},{10,11... | collective-permute-start | bytes 4423688 | tf_op jit(solution)/shard_map/ppermute | solution.py:452
  226.5 3.8 %shard_map.84 = (f32[15,96,128]{2,1,0:T(8,128)}, bf16[15,96,128]{2,1,0:T(8,128)(2,1)}, bf16[15,96,128]{2,1,0:T(8,128)(2,1)}, bf16[15,96,128]{2,1,0:T(8,128)(2,1)}) custom-call(s32[2]{0:T(128)} %pad_add_fusion.1.here_ref, bf16[4,15,96,128]{3,2,1,0:T(8,128)(2,1)} %get-tuple-element.37.keep_ref, bf16[4,15,96,128]{3,2,1,0:T(8,128)(2,1)} %copy-done.4), custom_call_target="tpu_custom_call" | custom-call | bytes 1048576 | tf_op jit(solution)/shard_map/pallas_call | solution.py:309
  237.4 4.7 %shard_map.78.refs_0_ = bf16[2,18,96,128]{3,2,1,0:T(8,128)(2,1)} custom-call(bf16[4,18,96,128]{3,2,1,0:T(8,128)(2,1)} %all-to-all-done.1.given_ref.refs_6_), custom_call_target="tpu_custom_call" | custom-call | bytes 1048576 | tf_op jit(solution)/shard_map/pallas_call | solution.py:332
  242.1 5.2 %shard_map.81.refs_1_ = bf16[2,18,96,128]{3,2,1,0:T(8,128)(2,1)} custom-call(bf16[8,18,96,128]{3,2,1,0:T(8,128)(2,1)} %all-to-all-done.2.given_ref), custom_call_target="tpu_custom_call" | custom-call | bytes 1048576 | tf_op jit(solution)/shard_map/pallas_call | solution.py:332
  247.3 5.4 %collective-permute-done.17.refs_4_ = bf16[15,96,128]{2,1,0:T(8,128)(2,1)S(1)} collective-permute-done((bf16[15,96,128]{2,1,0:T(8,128)(2,1)}, bf16[15,96,128]{2,1,0:T(8,128)(2,1)S(1)}, u32[]{:S(2)}, u32[]{:S(2)}) %collective-permute-start.17) | collective-permute-done | bytes 368672 | tf_op jit(solution)/shard_map/ppermute | solution.py:458
  253.5 5.6 %shard_map.85 = bf16[96,12288]{1,0:T(8,128)(2,1)} custom-call(s32[96]{0:T(128)} %slice.12.left_ref, s32[96]{0:T(128)} %slice.13.right_ref, s32[2]{0:T(128)} %pad_add_fusion.1.here_ref, bf16[2,18,96,128]{3,2,1,0:T(8,128)(2,1)} %shard_map.78.refs_0_, bf16[2,18,96,128]{3,2,1,0:T(8,128)(2,1)} %shard_map.81.refs_1_, f32[15,96,128]{2,1,0:T(8,128)} %get-tuple-element.39.refs_2_, ...), custom_call_target="tpu_custom_call" | custom-call | tf_op jit(solution)/shard_map/pallas_call | solution.py:393
  (97 shorter events, 46.9 us)
Async XLA Ops:
  1.8 21.4 %all-to-all-start = ((bf16[16,32,768]{2,1,0:T(8,128)(2,1)}), bf16[16,32,768]{2,1,0:T(8,128)(2,1)S(1)}, u32[]{:S(2)}, u32[]{:S(2)}) async-start(bf16[16,32,768]{2,1,0:T(8,128)(2,1)} %broadcast_in_dim.54), calls=%async_computation | async-start | bytes 1572864 | tf_op jit(solution)/shard_map/all_to_all | solution.py:413
  11.2 31.5 %copy-start.9 = (s32[192,4]{0,1:T(4,128)S(1)}, s32[192,4]{0,1:T(4,128)}, u32[]{:S(2)}) copy-start(s32[192,4]{0,1:T(4,128)} %param.10) | copy-start | bytes 9220
  39.7 51.0 %collective-permute-start.3 = (bf16[24,64,768]{2,1,0:T(8,128)(2,1)}, bf16[24,64,768]{2,1,0:T(8,128)(2,1)S(1)}, u32[]{:S(2)}, u32[]{:S(2)}) collective-permute-start(bf16[24,64,768]{2,1,0:T(8,128)(2,1)} %bitcast.14), channel_id=1, source_target_pairs={{0,24},{8,0},{16,8},{24,16},{32,56},{40,32},{48,40},{56,48},{64,88... | collective-permute-start | bytes 7077896 | tf_op jit(solution)/shard_map/ppermute | solution.py:435
  41.2 52.6 %collective-permute-start.2 = (bf16[24,64,768]{2,1,0:T(8,128)(2,1)}, bf16[24,64,768]{2,1,0:T(8,128)(2,1)}, u32[]{:S(2)}, u32[]{:S(2)}) collective-permute-start(bf16[24,64,768]{2,1,0:T(8,128)(2,1)} %bitcast.15), channel_id=1, source_target_pairs={{0,8},{8,16},{16,24},{24,0},{32,40},{40,48},{48,56},{56,32},{64,72... | collective-permute-start | bytes 7077896 | tf_op jit(solution)/shard_map/ppermute | solution.py:435
  41.2 52.6 %collective-permute-start.1 = (bf16[24,64,768]{2,1,0:T(8,128)(2,1)}, bf16[24,64,768]{2,1,0:T(8,128)(2,1)}, u32[]{:S(2)}, u32[]{:S(2)}) collective-permute-start(bf16[24,64,768]{2,1,0:T(8,128)(2,1)} %bitcast.16), channel_id=1, source_target_pairs={{0,96},{8,104},{16,112},{24,120},{32,0},{40,8},{48,16},{56,24},{64... | collective-permute-start | bytes 7077896 | tf_op jit(solution)/shard_map/ppermute | solution.py:435
  42.4 51.5 %collective-permute-start = (bf16[24,64,768]{2,1,0:T(8,128)(2,1)}, bf16[24,64,768]{2,1,0:T(8,128)(2,1)}, u32[]{:S(2)}, u32[]{:S(2)}) collective-permute-start(bf16[24,64,768]{2,1,0:T(8,128)(2,1)} %bitcast.17), channel_id=1, source_target_pairs={{0,32},{8,40},{16,48},{24,56},{32,64},{40,72},{48,80},{56,88},{64,... | collective-permute-start | bytes 7077896 | tf_op jit(solution)/shard_map/ppermute | solution.py:435
  102.6 49.9 %collective-permute-start.6 = (bf16[24,64,768]{2,1,0:T(8,128)(2,1)}, bf16[24,64,768]{2,1,0:T(8,128)(2,1)}, u32[]{:S(2)}, u32[]{:S(2)}) collective-permute-start(bf16[24,64,768]{2,1,0:T(8,128)(2,1)} %get-tuple-element.29), channel_id=1, source_target_pairs={{0,96},{8,104},{16,112},{24,120},{32,0},{40,8},{48,16},{56,24},{64... | collective-permute-start | bytes 7077896 | tf_op jit(solution)/shard_map/ppermute | solution.py:435
  104.0 51.7 %collective-permute-start.7 = (bf16[24,64,768]{2,1,0:T(8,128)(2,1)}, bf16[24,64,768]{2,1,0:T(8,128)(2,1)}, u32[]{:S(2)}, u32[]{:S(2)}) collective-permute-start(bf16[24,64,768]{2,1,0:T(8,128)(2,1)} %get-tuple-element.30), channel_id=1, source_target_pairs={{0,8},{8,16},{16,24},{24,0},{32,40},{40,48},{48,56},{56,32},{64,72... | collective-permute-start | bytes 7077896 | tf_op jit(solution)/shard_map/ppermute | solution.py:435
  104.0 51.7 %collective-permute-start.8 = (bf16[24,64,768]{2,1,0:T(8,128)(2,1)}, bf16[24,64,768]{2,1,0:T(8,128)(2,1)S(1)}, u32[]{:S(2)}, u32[]{:S(2)}) collective-permute-start(bf16[24,64,768]{2,1,0:T(8,128)(2,1)} %get-tuple-element.31), channel_id=1, source_target_pairs={{0,24},{8,0},{16,8},{24,16},{32,56},{40,32},{48,40},{56,48},{64,88... | collective-permute-start | bytes 7077896 | tf_op jit(solution)/shard_map/ppermute | solution.py:435
  106.7 51.1 %collective-permute-start.5 = (bf16[24,64,768]{2,1,0:T(8,128)(2,1)}, bf16[24,64,768]{2,1,0:T(8,128)(2,1)}, u32[]{:S(2)}, u32[]{:S(2)}) collective-permute-start(bf16[24,64,768]{2,1,0:T(8,128)(2,1)} %get-tuple-element.25.refs_4_), channel_id=1, source_target_pairs={{0,32},{8,40},{16,48},{24,56},{32,64},{40,72},{48,80},{56,88},{64,... | collective-permute-start | bytes 7077896 | tf_op jit(solution)/shard_map/ppermute | solution.py:435
  116.8 7.6 %collective-permute-start.4 = (bf16[4,18,96,128]{3,2,1,0:T(8,128)(2,1)}, bf16[4,18,96,128]{3,2,1,0:T(8,128)(2,1)S(1)}, u32[]{:S(2)}, u32[]{:S(2)}) collective-permute-start(bf16[4,18,96,128]{3,2,1,0:T(8,128)(2,1)} %get-tuple-element.28), channel_id=1, source_target_pairs={{0,1},{1,0},{2,3},{3,2},{4,5},{5,4},{6,7},{7,6},{8,9},{9,8},{10,11... | collective-permute-start | bytes 5308424 | tf_op jit(solution)/shard_map/ppermute | solution.py:452
  130.8 53.9 %all-to-all-start.1 = ((bf16[4,18,96,128]{3,2,1,0:T(8,128)(2,1)}), bf16[4,18,96,128]{3,2,1,0:T(8,128)(2,1)}, u32[]{:S(2)}, u32[]{:S(2)}) async-start(bf16[4,18,96,128]{3,2,1,0:T(8,128)(2,1)} %shard_map.77.refs_4_), calls=%async_computation.1 | async-start | bytes 3538944 | tf_op jit(solution)/shard_map/all_to_all | solution.py:463
  164.6 20.0 %collective-permute-start.13 = (bf16[6,64,768]{2,1,0:T(8,128)(2,1)}, bf16[6,64,768]{2,1,0:T(8,128)(2,1)}, u32[]{:S(2)}, u32[]{:S(2)}) collective-permute-start(bf16[6,64,768]{2,1,0:T(8,128)(2,1)} %get-tuple-element.36), channel_id=1, source_target_pairs={{0,16},{8,24},{16,0},{24,8},{32,48},{40,56},{48,32},{56,40},{64,80... | collective-permute-start | bytes 1769480 | tf_op jit(solution)/shard_map/ppermute | solution.py:435
  166.1 39.0 %collective-permute-start.10 = (bf16[12,64,768]{2,1,0:T(8,128)(2,1)}, bf16[12,64,768]{2,1,0:T(8,128)(2,1)S(1)}, u32[]{:S(2)}, u32[]{:S(2)}) collective-permute-start(bf16[12,64,768]{2,1,0:T(8,128)(2,1)} %get-tuple-element.33), channel_id=1, source_target_pairs={{0,24},{8,0},{16,8},{24,16},{32,56},{40,32},{48,40},{56,48},{64,88... | collective-permute-start | bytes 3538952 | tf_op jit(solution)/shard_map/ppermute | solution.py:435
  166.8 38.4 %collective-permute-start.11 = (bf16[12,64,768]{2,1,0:T(8,128)(2,1)}, bf16[12,64,768]{2,1,0:T(8,128)(2,1)S(1)}, u32[]{:S(2)}, u32[]{:S(2)}) collective-permute-start(bf16[12,64,768]{2,1,0:T(8,128)(2,1)} %get-tuple-element.34), channel_id=1, source_target_pairs={{0,32},{8,40},{16,48},{24,56},{32,64},{40,72},{48,80},{56,88},{64,... | collective-permute-start | bytes 3538952 | tf_op jit(solution)/shard_map/ppermute | solution.py:435
  168.0 37.2 %collective-permute-start.12 = (bf16[12,64,768]{2,1,0:T(8,128)(2,1)}, bf16[12,64,768]{2,1,0:T(8,128)(2,1)S(1)}, u32[]{:S(2)}, u32[]{:S(2)}) collective-permute-start(bf16[12,64,768]{2,1,0:T(8,128)(2,1)} %get-tuple-element.35), channel_id=1, source_target_pairs={{0,96},{8,104},{16,112},{24,120},{32,0},{40,8},{48,16},{56,24},{64... | collective-permute-start | bytes 3538952 | tf_op jit(solution)/shard_map/ppermute | solution.py:435
  169.4 36.8 %collective-permute-start.9 = (bf16[12,64,768]{2,1,0:T(8,128)(2,1)}, bf16[12,64,768]{2,1,0:T(8,128)(2,1)}, u32[]{:S(2)}, u32[]{:S(2)}) collective-permute-start(bf16[12,64,768]{2,1,0:T(8,128)(2,1)} %get-tuple-element.32.refs_4_), channel_id=1, source_target_pairs={{0,8},{8,16},{16,24},{24,0},{32,40},{40,48},{48,56},{56,32},{64,72... | collective-permute-start | bytes 3538952 | tf_op jit(solution)/shard_map/ppermute | solution.py:435
  184.6 18.7 %collective-permute-start.14 = (bf16[6,64,768]{2,1,0:T(8,128)(2,1)}, bf16[6,64,768]{2,1,0:T(8,128)(2,1)}, u32[]{:S(2)}, u32[]{:S(2)}) collective-permute-start(bf16[6,64,768]{2,1,0:T(8,128)(2,1)} %shard_map.82), channel_id=1, source_target_pairs={{0,64},{8,72},{16,80},{24,88},{32,96},{40,104},{48,112},{56,120},{... | collective-permute-start | bytes 1769480 | tf_op jit(solution)/shard_map/ppermute | solution.py:435
  184.7 57.4 %all-to-all-start.2 = ((bf16[8,18,96,128]{3,2,1,0:T(8,128)(2,1)}), bf16[8,18,96,128]{3,2,1,0:T(8,128)(2,1)}, u32[]{:S(2)}, u32[]{:S(2)}) async-start(bf16[8,18,96,128]{3,2,1,0:T(8,128)(2,1)} %shard_map.80.refs_1_), calls=%async_computation.2 | async-start | bytes 7077888 | tf_op jit(solution)/shard_map/all_to_all | solution.py:498
  218.6 17.4 %copy-start.11 = (pred[192]{0:T(512)(128)(4,1)S(1)}, pred[192]{0:T(512)(128)(4,1)}, u32[]{:S(2)}) copy-start(pred[192]{0:T(512)(128)(4,1)} %copy-done.10) | copy-start | bytes 580
  218.6 6.8 %collective-permute-start.15 = (bf16[4,15,96,128]{3,2,1,0:T(8,128)(2,1)}, bf16[4,15,96,128]{3,2,1,0:T(8,128)(2,1)S(1)}, u32[]{:S(2)}, u32[]{:S(2)}) collective-permute-start(bf16[4,15,96,128]{3,2,1,0:T(8,128)(2,1)} %get-tuple-element.38), channel_id=1, source_target_pairs={{0,1},{1,0},{2,3},{3,2},{4,5},{5,4},{6,7},{7,6},{8,9},{9,8},{10,11... | collective-permute-start | bytes 4423688 | tf_op jit(solution)/shard_map/ppermute | solution.py:452
  230.4 16.9 %collective-permute-start.16 = (bf16[15,96,128]{2,1,0:T(8,128)(2,1)}, bf16[15,96,128]{2,1,0:T(8,128)(2,1)S(1)}, u32[]{:S(2)}, u32[]{:S(2)}) collective-permute-start(bf16[15,96,128]{2,1,0:T(8,128)(2,1)} %get-tuple-element.40), channel_id=1, source_target_pairs={{0,4},{1,5},{2,6},{3,7},{4,0},{5,1},{6,2},{7,3},{8,12},{9,13},{10,... | collective-permute-start | bytes 1105928 | tf_op jit(solution)/shard_map/ppermute | solution.py:458
  233.1 19.5 %collective-permute-start.17 = (bf16[15,96,128]{2,1,0:T(8,128)(2,1)}, bf16[15,96,128]{2,1,0:T(8,128)(2,1)S(1)}, u32[]{:S(2)}, u32[]{:S(2)}) collective-permute-start(bf16[15,96,128]{2,1,0:T(8,128)(2,1)} %get-tuple-element.41), channel_id=1, source_target_pairs={{0,2},{1,3},{2,4},{3,5},{4,6},{5,7},{6,0},{7,1},{8,10},{9,11},{10,... | collective-permute-start | bytes 1105928 | tf_op jit(solution)/shard_map/ppermute | solution.py:458
  233.4 19.2 %collective-permute-start.18 = (bf16[15,96,128]{2,1,0:T(8,128)(2,1)}, bf16[15,96,128]{2,1,0:T(8,128)(2,1)S(1)}, u32[]{:S(2)}, u32[]{:S(2)}) collective-permute-start(bf16[15,96,128]{2,1,0:T(8,128)(2,1)} %get-tuple-element.42), channel_id=1, source_target_pairs={{0,6},{1,7},{2,0},{3,1},{4,2},{5,3},{6,4},{7,5},{8,14},{9,15},{10,... | collective-permute-start | bytes 1105928 | tf_op jit(solution)/shard_map/ppermute | solution.py:458
  (14 other events, 47.8 us)
